TPU v7x, 128 devices: a whole 4x4x4 slice. The times are simulated.
128 devices in a mesh: grp: 4 (over y_lo, core), mem: 32 (over x, z, y_hi).
Axes of the slice: x: 4, y: 4 (y_hi: 2, y_lo: 2; y = y_hi * 2 + y_lo), z: 4, core: 2. Of those that a mesh axis runs over, the one named last changes fastest.
Arguments:
- video: bfloat16 [128, 32, 32, 1024], P('mem', 'grp'), may hold values from -6 to 6
- w_triple: bfloat16 [2, 1024, 3072], replicated, may hold values from -0.75 to 0.75, as said below
- w_out: bfloat16 [2, 1024, 1024], replicated, may hold values from -0.1875 to 0.1875
Outputs:
- result: bfloat16 [128, 32, 32, 1024], P('mem', 'grp')
Inputs may be any that keep to these rules, and one draw needn't show every extreme that they name: `w_triple`: entries of order 1024 ** -0.5, independent between columns of values.
All inputs are finite; a program needn't handle non-finite values.
Results may differ from a plain program's by a relative error of at most 0.008.
Values may be sent and summed in bfloat16 or wider, within the bound.
No kernel may reach another device: no remote copies, remote signals or barrier semaphores. Data moves between devices by JAX's collectives and lax.ppermute only.
A program may use at most 128 MiB of HBM per device.

v0:
```python
import jax
import jax.numpy as jnp
from jax import lax
from jax.sharding import PartitionSpec as P

HEADS = 16
HEAD = 64


eps = 1e-06
time_forms = ("sabhe,tabhe->abhst", "abhst,tabhe->sabhe")
height_forms = ("asbhe,atbhe->abhst", "abhst,atbhe->asbhe")


def attend_local(triple, forms):
    lead = triple.shape[:-1]
    width = triple.shape[-1] // 3
    pieces = triple.reshape(lead + (3, HEADS, HEAD))
    query = pieces[..., 0, :, :]
    keys = pieces[..., 1, :, :]
    values = pieces[..., 2, :, :]
    scores = jnp.einsum(forms[0], query, keys, preferred_element_type=jnp.float32) * (
        1.0 / HEAD**0.5
    )
    top = jnp.max(scores, axis=-1, keepdims=True)
    expo = jnp.exp(scores - top)
    probs = (expo / jnp.sum(expo, axis=-1, keepdims=True)).astype(jnp.bfloat16)
    context = jnp.einsum(forms[1], probs, values, preferred_element_type=jnp.float32)
    return context.astype(jnp.bfloat16).reshape(lead + (width,))


def make_triple(state, weight_in):
    width = state.shape[-1]
    floats = state.astype(jnp.float32)
    normed = (floats * lax.rsqrt(jnp.mean(floats * floats, axis=-1, keepdims=True) + eps)).astype(
        jnp.bfloat16
    )
    triple = jnp.dot(normed.reshape(-1, width), weight_in, preferred_element_type=jnp.float32)
    return triple.astype(jnp.bfloat16).reshape(state.shape[:-1] + (3 * width,))


def add_update(state, context, weight_back):
    width = state.shape[-1]
    update = jnp.dot(context.reshape(-1, width), weight_back, preferred_element_type=jnp.float32)
    return (state.astype(jnp.float32) + update.reshape(state.shape)).astype(jnp.bfloat16)


def on_device(video, w_triple, w_out):
    triple = make_triple(video, w_triple[0])
    context = attend_local(
        lax.all_to_all(triple, "mem", split_axis=2, concat_axis=0, tiled=True), time_forms
    )
    context = lax.all_to_all(context, "mem", split_axis=0, concat_axis=2, tiled=True)
    after_time = add_update(video, context, w_out[0])
    triple = make_triple(after_time, w_triple[1])
    context_rows = attend_local(
        lax.all_to_all(triple, "grp", split_axis=2, concat_axis=1, tiled=True), height_forms
    )
    context = lax.all_to_all(context_rows, "grp", split_axis=1, concat_axis=2, tiled=True)
    return add_update(after_time, context, w_out[1])


def solution(mesh):
    return jax.shard_map(
        on_device,
        mesh=mesh,
        in_specs=(P("mem", "grp", None, None), P(), P()),
        out_specs=P("mem", "grp", None, None),
        check_vma=False,
    )
```

profile of v0, /device:TPU:1, one launch (start us, length us, event | category | flops | bytes accessed | tf_op | source)
XLA Modules:
  0.0 384.3 jit_solution(9550029064572870025)
XLA Ops:
  0.0 2.1 fusion.20
  2.1 2.0 fusion.21
  4.1 9.7 %fusion.10 = bf16[1024,3072]{1,0:T(8,128)(2,1)S(1)} fusion(bf16[1024,1024]{1,0:T(8,128)(2,1)S(1)} %bitcast.106, bf16[2,1024,3072]{2,1,0:T(8,128)(2,1)} %param.4), kind=kOutput, calls=%fused_computation.22 | convolution fusion | flops 6445596672 | bytes 14680064 | tf_op jit(solution)/shard_map/dot_general | solution.py:38
  13.8 3.4 copy.33
  17.2 85.5 %all_to_all.60 = bf16[4,8,32,3072]{3,1,0,2:T(8,128)(2,1)} all-to-all(bf16[4,8,32,3072]{3,1,0,2:T(8,128)(2,1)S(1)} %copy.33), channel_id=1, replica_groups=mesh['grp'=4,'mem'=32] {'mem'}, dimensions={2} | all-to-all | bytes 12582912 | tf_op jit(solution)/shard_map/all_to_all | solution.py:51
  102.7 15.9 %reshape.88 = bf16[128,8,1,3,16,64]{5,4,3,1,0,2:T(8,128)(2,1)} reshape(bf16[32,4,8,1,3072]{4,2,1,0,3:T(8,128)(2,1)} %bitcast.100) | data formatting | bytes 12582912 | tf_op jit(solution)/shard_map/reshape | solution.py:18
  118.7 9.4 %fusion.60 = (bf16[128,8,1,1,16,64]{5,4,3,1,0,2:T(8,128)(2,1)}, bf16[128,8,1,1,16,64]{5,4,3,1,0,2:T(8,128)(2,1)}, bf16[128,8,1,1,16,64]{5,4,3,1,0,2:T(8,128)(2,1)}) fusion(bf16[128,8,1,3,16,64]{5,4,3,1,0,2:T(8,128)(2,1)} %reshape.88), kind=kLoop, calls=%fused_computation.60 | loop fusion | bytes 12582912 | tf_op jit(solution)/shard_map/slice | solution.py:21
  128.1 6.5 %copy.59 = bf16[128,8,1,1,16,64]{0,5,4,1,3,2:T(8,128)(2,1)} copy(bf16[128,8,1,1,16,64]{5,4,3,1,0,2:T(8,128)(2,1)} %get-tuple-element.8) | data formatting | bytes 4194304
  134.6 5.6 %copy.60 = bf16[128,8,1,1,16,64]{0,5,4,1,3,2:T(8,128)(2,1)S(1)} copy(bf16[128,8,1,1,16,64]{5,4,3,1,0,2:T(8,128)(2,1)} %get-tuple-element.9) | data formatting | bytes 4194304
  140.2 6.5 %copy.61 = bf16[128,8,1,1,16,64]{0,5,4,1,3,2:T(8,128)(2,1)} copy(bf16[128,8,1,1,16,64]{5,4,3,1,0,2:T(8,128)(2,1)} %get-tuple-element.10) | data formatting | bytes 4194304
  146.8 2.9 fusion.39
  149.7 0.0 copy-start.1
  149.7 7.8 %fusion.61 = (f32[8,16,128]{2,1,0:T(8,128)S(1)}, f32[8,16,128,128]{2,3,1,0:T(8,128)S(1)}) fusion(f32[8,16,128,128]{2,3,1,0:T(8,128)S(1)} %fusion.39), kind=kOutput, calls=%fused_computation.61 | output fusion | flops 8388735 | bytes 16842752 | tf_op jit(solution)/shard_map/sub | solution.py:26
  157.6 0.0 copy-done.1
  157.6 2.6 fusion.46
  160.1 0.0 copy-start
  160.1 4.3 %copy.38 = bf16[128,8,1,1024]{3,1,2,0:T(8,128)(2,1)} copy(bf16[128,8,1,1024]{0,3,1,2:T(8,128)(2,1)} %bitcast.103) | data formatting | bytes 4194304 | tf_op jit(solution)/shard_map/reshape | solution.py:29
  164.5 0.0 copy-start.4
  164.5 34.4 %all_to_all.61 = bf16[128,8,1,1024]{3,1,2,0:T(8,128)(2,1)S(1)} all-to-all(bf16[128,8,1,1024]{3,1,2,0:T(8,128)(2,1)} %copy.38), channel_id=1, replica_groups=mesh['grp'=4,'mem'=32] {'mem'}, dimensions={0} | all-to-all | bytes 4194304 | tf_op jit(solution)/shard_map/all_to_all | solution.py:53
  198.9 0.0 copy-done
  198.9 0.0 copy-done.4
  198.9 2.8 fusion.23
  201.7 0.0 copy-start.2
  201.7 0.4 fusion.24
  202.2 0.9 copy-done.2
  203.1 9.7 %fusion.13 = bf16[1024,3072]{1,0:T(8,128)(2,1)S(1)} fusion(bf16[1024,1024]{1,0:T(8,128)(2,1)S(1)} %bitcast.107, bf16[2,1024,3072]{2,1,0:T(8,128)(2,1)} %param.4), kind=kOutput, calls=%fused_computation.23 | convolution fusion | flops 6445596672 | bytes 14680064 | tf_op jit(solution)/shard_map/dot_general | solution.py:38
  212.7 3.4 copy.40
  216.2 75.6 %all_to_all.62 = bf16[4,8,32,3072]{3,1,0,2:T(8,128)(2,1)S(1)} all-to-all(bf16[4,8,32,3072]{3,1,0,2:T(8,128)(2,1)S(1)} %copy.40), channel_id=1, replica_groups=mesh['grp'=4,'mem'=32] {'grp'}, dimensions={2} | all-to-all | bytes 12582912 | tf_op jit(solution)/shard_map/all_to_all | solution.py:57
  291.7 6.8 %copy.42 = bf16[4,4,8,8,3072]{4,3,2,1,0:T(8,128)(2,1)} copy(bf16[4,4,8,8,3072]{4,2,0,3,1:T(8,128)(2,1)S(1)} %bitcast.99) | data formatting | bytes 12582912 | tf_op jit(solution)/shard_map/all_to_all | solution.py:57
  298.6 15.9 %reshape.95 = bf16[4,32,8,3,16,64]{5,4,3,2,1,0:T(8,128)(2,1)} reshape(bf16[4,4,8,8,3072]{4,3,2,1,0:T(8,128)(2,1)} %copy.42) | data formatting | bytes 12582912 | tf_op jit(solution)/shard_map/reshape | solution.py:18
  314.5 8.1 %fusion.59 = (bf16[4,32,8,1,16,64]{5,4,3,2,1,0:T(8,128)(2,1)}, bf16[4,32,8,1,16,64]{5,4,3,2,1,0:T(8,128)(2,1)S(1)}, bf16[4,32,8,1,16,64]{5,4,3,2,1,0:T(8,128)(2,1)S(1)}) fusion(bf16[4,32,8,3,16,64]{5,4,3,2,1,0:T(8,128)(2,1)} %reshape.95), kind=kLoop, calls=%fused_computation.59 | loop fusion | bytes 12582912 | tf_op jit(solution)/shard_map/slice | solution.py:21
  322.6 5.4 %fusion.27 = f32[4,8,16,32,32]{3,4,2,1,0:T(8,128)S(1)} fusion(bf16[4,32,8,1,16,64]{5,4,3,2,1,0:T(8,128)(2,1)S(1)} %get-tuple-element.7, bf16[4,32,8,1,16,64]{5,4,3,2,1,0:T(8,128)(2,1)S(1)} %get-tuple-element.6), kind=kOutput, calls=%fused_computation.32 | convolution fusion | flops 67108864 | bytes 6291456 | tf_op jit(solution)/shard_map/asbhe,atbhe->abhst/dot_general | solution.py:22
  327.9 5.0 %fusion.62 = (f32[4,8,16,32]{3,2,1,0:T(8,128)S(1)}, f32[4,8,16,32,32]{3,4,2,1,0:T(8,128)}) fusion(f32[4,8,16,32,32]{3,4,2,1,0:T(8,128)S(1)} %fusion.27), kind=kOutput, calls=%fused_computation.62 | output fusion | flops 2097183 | bytes 4259840 | tf_op jit(solution)/shard_map/sub | solution.py:26
  333.0 8.2 %convert_bitcast_fusion = bf16[4,32,8,16,64]{4,1,3,2,0:T(8,128)(2,1)S(1)} fusion(f32[4,8,16,32,32]{3,4,2,1,0:T(8,128)} %get-tuple-element.16, f32[4,8,16,32]{3,2,1,0:T(8,128)S(1)} %get-tuple-element.15, bf16[4,32,8,1,16,64]{5,4,3,2,1,0:T(8,128)(2,1)} %get-tuple-element.5), kind=kOutput, calls=%fused_computation.35 | convolution fusion | flops 69206016 | bytes 6356992 | tf_op jit(solution)/shard_map/abhst,atbhe->asbhe/dot_general | solution.py:28
  341.2 3.6 copy.56
  344.7 5.5 %reshape.99 = bf16[4,32,8,1024]{3,2,0,1:T(8,128)(2,1)S(1)} reshape(bf16[4,32,8,16,64]{4,3,2,0,1:T(8,128)(2,1)} %copy.56) | data formatting | bytes 4194304 | tf_op jit(solution)/shard_map/reshape | solution.py:29
  350.2 0.0 copy-start.3
  350.2 28.3 %all_to_all.63 = bf16[4,32,8,1024]{3,2,0,1:T(8,128)(2,1)S(1)} all-to-all(bf16[4,32,8,1024]{3,2,0,1:T(8,128)(2,1)S(1)} %reshape.99), channel_id=1, replica_groups=mesh['grp'=4,'mem'=32] {'grp'}, dimensions={1} | all-to-all | bytes 4194304 | tf_op jit(solution)/shard_map/all_to_all | solution.py:59
  378.5 0.0 copy-done.3
  378.5 5.2 %fusion.25 = bf16[4,8,32,1024]{3,2,1,0:T(8,128)(2,1)} fusion(bf16[4,8,32,1024]{3,2,1,0:T(8,128)(2,1)S(1)} %copy-done.3, bf16[2,1024,1024]{2,1,0:T(8,128)(2,1)} %param.5, bf16[4,8,4,8,1024]{4,3,0,1,2:T(8,128)(2,1)S(1)} %bitcast.105), kind=kOutput, calls=%fused_computation.29 | convolution fusion | flops 2150629376 | bytes 8388608 | tf_op jit(solution)/shard_map/dot_general | solution.py:44
  (2 shorter events, 0.0 us)
Async XLA Ops:
  149.7 7.9 %copy-start.1 = (bf16[128,8,1,1,16,64]{0,5,4,1,3,2:T(8,128)(2,1)S(1)}, bf16[128,8,1,1,16,64]{0,5,4,1,3,2:T(8,128)(2,1)}, u32[]{:S(2)}) copy-start(bf16[128,8,1,1,16,64]{0,5,4,1,3,2:T(8,128)(2,1)} %copy.59) | copy-start | bytes 6291460
  160.1 38.8 %copy-start = (bf16[4,8,32,1024]{3,2,1,0:T(8,128)(2,1)S(1)}, bf16[4,8,32,1024]{3,2,1,0:T(8,128)(2,1)}, u32[]{:S(2)}) copy-start(bf16[4,8,32,1024]{3,2,1,0:T(8,128)(2,1)} %param.3) | copy-start | bytes 6291460
  164.5 34.4 %copy-start.4 = (bf16[2,1024,1024]{2,1,0:T(8,128)(2,1)S(1)}, bf16[2,1024,1024]{2,1,0:T(8,128)(2,1)}, u32[]{:S(2)}) copy-start(bf16[2,1024,1024]{2,1,0:T(8,128)(2,1)} %param.5) | copy-start | bytes 12582916
  201.7 1.3 copy-start.2
  350.2 28.3 %copy-start.3 = (bf16[4,8,32,1024]{3,2,1,0:T(8,128)(2,1)S(1)}, bf16[4,8,32,1024]{3,2,1,0:T(8,128)(2,1)}, u32[]{:S(2)}) copy-start(bf16[4,8,32,1024]{3,2,1,0:T(8,128)(2,1)} %copy-done.2) | copy-start | bytes 6291460
where the time goes:
time: 391 us; the launch traced here: 384 us
  blocking collectives  224 us (57%)
  local copies, waits for them, and re-layouts  96 us (25%)
  matrix products  46.4 us (12%)
  other arithmetic  17.4 us (4%)
    all_to_all x1, blocking collectives, on_device(): lax.all_to_all(triple, 'mem', split_axis=2, concat_axis=0, tiled=True)  85.5 us
    all_to_all x1, blocking collectives, on_device(): lax.all_to_all(triple, 'grp', split_axis=2, concat_axis=1, tiled=True)  75.6 us
    all_to_all x1, blocking collectives, on_device(): lax.all_to_all(context, 'mem', split_axis=0, concat_axis=2, tiled=True)  34.4 us
    reshape x2, local copies, waits for them, and re-layouts, attend_local(): pieces = triple.reshape(lead + (3, HEADS, HEAD))  31.9 us
    all_to_all x1, blocking collectives, on_device(): lax.all_to_all(context_rows, 'grp', split_axis=1, concat_axis=2, tiled=True)  28.3 us
    unnamed x13, local copies, waits for them, and re-layouts  19.6 us
    dot_general x2, matrix products, make_triple(): jnp.dot(normed.reshape(-1, width), weight_in, preferred_element_type=jnp....  19.3 us
    slice x2, local copies, waits for them, and re-layouts, attend_local(): values = pieces[..., 2, :, :]  17.5 us

commit v1 on v0

v1 whole, which is shorter than its diff:
```python
import functools
import math

import jax
import jax.numpy as jnp
from jax import lax
from jax.experimental import pallas as pl
from jax.experimental.pallas import tpu as pltpu
from jax.sharding import PartitionSpec as P

D = 1024
HEADS = 16
HEAD = 64
EPS = 1e-06
PAIRS = HEADS // 2
SCALE = math.log2(math.e) / math.sqrt(HEAD)
BF = jnp.bfloat16
F32 = jnp.float32

LINE = 128
GROUP = 256


def relayout_kernel(perm_ref, x_ref, o_ref):
    x = x_ref[...].reshape(GROUP, D)
    y = jnp.dot(perm_ref[...], x, preferred_element_type=F32).astype(BF)
    o_ref[...] = y.reshape(o_ref.shape)


def permutation(rows, columns):
    return (rows[:, None] == columns[None, :]).astype(BF)


def to_columns(video):
    o = jnp.arange(GROUP)
    want = (o % 4) * 64 + ((o // 4) % 2) * 32 + o // 8
    perm = permutation(want, o)
    return pl.pallas_call(
        relayout_kernel,
        grid=(4,),
        in_specs=[
            pl.BlockSpec((GROUP, GROUP), lambda t: (0, 0)),
            pl.BlockSpec((4, 2, 32, D), lambda t: (0, t, 0, 0)),
        ],
        out_specs=pl.BlockSpec((32, None, 8, D), lambda t: (0, t, 0, 0)),
        out_shape=jax.ShapeDtypeStruct((32, 4, 8, D), BF),
        name="to_columns",
    )(perm, video)


def to_tokens(columns):
    o = jnp.arange(GROUP)
    want = (o % 32) * 8 + o // 32
    perm = permutation(want, o)
    return pl.pallas_call(
        relayout_kernel,
        grid=(4,),
        in_specs=[
            pl.BlockSpec((GROUP, GROUP), lambda j: (0, 0)),
            pl.BlockSpec((32, None, 8, D), lambda j: (0, j, 0, 0)),
        ],
        out_specs=pl.BlockSpec((None, 8, 32, D), lambda j: (j, 0, 0, 0)),
        out_shape=jax.ShapeDtypeStruct((4, 8, 32, D), BF),
        name="to_tokens",
    )(perm, columns)


def load_tokens(perm, pieces, xp_ref, normed_ref, at):
    x = jnp.concatenate(pieces, axis=0) if len(pieces) > 1 else pieces[0]
    x = jnp.dot(perm, x, preferred_element_type=F32)
    xp_ref[pl.ds(at, GROUP), :] = x.astype(BF)
    power = jnp.mean(x * x, axis=-1, keepdims=True)
    normed_ref[pl.ds(at, GROUP), :] = (x * lax.rsqrt(power + EPS)).astype(BF)


def project(normed_ref, w_ref, qkv_ref, step=512):
    @pl.loop(0, 3 * D // step)
    def _(n):
        at = pl.multiple_of(n * step, step)
        acc = jnp.dot(normed_ref[...], w_ref[:, pl.ds(at, step)], preferred_element_type=F32)
        qkv_ref[:, pl.ds(at, step)] = acc.astype(BF)


def attend(qkv_ref, ctx_ref, masked):
    tokens = qkv_ref.shape[0]
    low = (lax.broadcasted_iota(jnp.int32, (LINE, LINE), 1) < HEAD).astype(F32)
    low, high = low.astype(BF), (1.0 - low).astype(BF)
    if masked:
        a = lax.broadcasted_iota(jnp.int32, (2 * LINE, LINE), 0) % LINE // 32
        b = lax.broadcasted_iota(jnp.int32, (2 * LINE, LINE), 1) // 32
        same = a == b

    @pl.loop(0, tokens // LINE)
    def _(i):
        rows = pl.ds(pl.multiple_of(i * LINE, LINE), LINE)
        for p in range(PAIRS):
            q = qkv_ref[rows, p * 128 : p * 128 + 128]
            k = qkv_ref[rows, D + p * 128 : D + p * 128 + 128]
            v = qkv_ref[rows, 2 * D + p * 128 : 2 * D + p * 128 + 128]
            q = jnp.concatenate([q * low, q * high], axis=0)
            s = lax.dot_general(q, k, (((1,), (1,)), ((), ())), preferred_element_type=F32)
            if masked:
                s = jnp.where(same, s, -1e30)
            top = jnp.max(s, axis=-1, keepdims=True)
            e = jnp.exp2((s - top) * SCALE).astype(BF)
            e = jnp.concatenate([e[:LINE], e[LINE:]], axis=1)
            v = jnp.concatenate(
                [
                    jnp.concatenate([v * low, low], axis=1),
                    jnp.concatenate([v * high, high], axis=1),
                ],
                axis=0,
            )
            o = jnp.dot(e, v, preferred_element_type=F32)
            ctx_ref[rows, p * 128 : p * 128 + 128] = (o[:, :128] / o[:, 128:]).astype(BF)


def update(xp_ref, ctx_ref, wo_ref, y_ref, step=512):
    for at in range(0, D, step):
        acc = jnp.dot(ctx_ref[...], wo_ref[:, at : at + step], preferred_element_type=F32)
        y_ref[:, at : at + step] = (xp_ref[:, at : at + step].astype(F32) + acc).astype(BF)


def time_kernel(perm_ref, x_ref, w_ref, wo_ref, *refs):
    outs, (xp_ref, normed_ref, qkv_ref, ctx_ref) = refs[:4], refs[4:]
    perm = perm_ref[...]
    groups = x_ref.shape[1]
    for t in range(groups):
        load_tokens(perm, [x_ref[:, t].reshape(GROUP, D)], xp_ref, normed_ref, t * GROUP)
    project(normed_ref, w_ref, qkv_ref)
    attend(qkv_ref, ctx_ref, False)
    update(xp_ref, ctx_ref, wo_ref, normed_ref)
    for r in range(2 * groups):
        for s in range(4):
            at = (r * 4 + s) * 32
            outs[s][r] = normed_ref[at : at + 32, :]


def scratch(tokens):
    return [
        pltpu.VMEM((tokens, D), BF),
        pltpu.VMEM((tokens, D), BF),
        pltpu.VMEM((tokens, 3 * D), BF),
        pltpu.VMEM((tokens, D), BF),
    ]


def block_cost(tokens):
    return pl.CostEstimate(
        flops=2 * tokens * D * D * 4 + 4 * tokens * 128 * D,
        bytes_accessed=8 * D * D + 4 * tokens * D,
        transcendentals=tokens * 128 * HEADS,
    )


def time_block(perm, lines, w_triple, w_out, k, groups):
    tokens = groups * GROUP
    shape = jax.ShapeDtypeStruct((2 * groups, 32, D), BF)
    return pl.pallas_call(
        time_kernel,
        grid=(1,),
        in_specs=[
            pl.BlockSpec((GROUP, GROUP), lambda i: (0, 0)),
            pl.BlockSpec((32, groups, 8, D), lambda i: (0, k, 0, 0)),
            pl.BlockSpec((None, D, 3 * D), lambda i: (0, 0, 0)),
            pl.BlockSpec((None, D, D), lambda i: (0, 0, 0)),
        ],
        out_specs=[pl.BlockSpec((2 * groups, 32, D), lambda i: (0, 0, 0))] * 4,
        out_shape=[shape] * 4,
        scratch_shapes=scratch(tokens),
        cost_estimate=block_cost(tokens),
        compiler_params=pltpu.CompilerParams(vmem_limit_bytes=48 * 2**20),
        name=f"time_block_{k}",
    )(perm, lines, w_triple, w_out)


def height_kernel(n, perm_ref, *refs):
    pieces, (w_ref, wo_ref, y_ref), (xp_ref, normed_ref, qkv_ref, ctx_ref) = (
        refs[:n],
        refs[n : n + 3],
        refs[n + 3 :],
    )
    perm = perm_ref[...]
    groups = y_ref.shape[0] // 8
    for t in range(groups):
        parts = [
            piece[r, t * 8 : t * 8 + 8, :] for piece in pieces for r in range(piece.shape[0])
        ]
        load_tokens(perm, parts, xp_ref, normed_ref, t * GROUP)
    project(normed_ref, w_ref, qkv_ref)
    attend(qkv_ref, ctx_ref, True)
    update(xp_ref, ctx_ref, wo_ref, normed_ref)
    y_ref[...] = normed_ref[...].reshape(y_ref.shape)


def height_block(perm, pieces, w_triple, w_out, k, groups):
    tokens = groups * GROUP
    rows = pieces[0].shape[0]
    return pl.pallas_call(
        functools.partial(height_kernel, len(pieces)),
        grid=(1,),
        in_specs=[pl.BlockSpec((GROUP, GROUP), lambda i: (0, 0))]
        + [pl.BlockSpec((rows, 8 * groups, D), lambda i: (0, k, 0))] * len(pieces)
        + [
            pl.BlockSpec((None, D, 3 * D), lambda i: (1, 0, 0)),
            pl.BlockSpec((None, D, D), lambda i: (1, 0, 0)),
        ],
        out_specs=pl.BlockSpec((8 * groups, 32, D), lambda i: (0, 0, 0)),
        out_shape=jax.ShapeDtypeStruct((8 * groups, 32, D), BF),
        scratch_shapes=scratch(tokens),
        cost_estimate=block_cost(tokens),
        compiler_params=pltpu.CompilerParams(vmem_limit_bytes=48 * 2**20),
        name=f"height_block_{k}",
    )(perm, *pieces, w_triple, w_out)


CHUNKS0 = 2
CHUNKS1 = 1


def on_device(video, w_triple, w_out):
    g = lax.axis_index("grp")
    o = jnp.arange(GROUP)
    want = (o % 32) * 8 + (o // 128) * 4 + (((o // 32) % 4) ^ g)
    perm0 = permutation(want, o)
    rows = 8 // CHUNKS0
    m, rg, r = o // 32, (o // 8) % 4, o % 8
    want = (((r // rows) * 4 + (rg ^ g)) * rows + r % rows) * 8 + m
    perm1 = permutation(want, o)

    lines = lax.all_to_all(to_columns(video), "mem", split_axis=0, concat_axis=0, tiled=True)
    pieces = []
    for k in range(CHUNKS0):
        outs = time_block(perm0, lines, w_triple, w_out, k, 4 // CHUNKS0)
        pieces.append(outs[0])
        for s in range(1, 4):
            pieces.append(lax.ppermute(outs[s], "grp", [(i, i ^ s) for i in range(4)]))
    done = [
        height_block(perm1, pieces, w_triple, w_out, k, 4 // CHUNKS1) for k in range(CHUNKS1)
    ]
    done = jnp.concatenate(done, axis=0) if CHUNKS1 > 1 else done[0]
    done = lax.all_to_all(
        done.reshape(128, 8, D), ("mem", "grp"), split_axis=0, concat_axis=0, tiled=True
    )
    return to_tokens(done.reshape(32, 4, 8, D))


def solution(mesh):
    return jax.shard_map(
        on_device,
        mesh=mesh,
        in_specs=(P("mem", "grp", None, None), P(), P()),
        out_specs=P("mem", "grp", None, None),
        check_vma=False,
    )
```

time: 391 us -> 151 us (0.39); the launches traced: 384 us -> 151 us
  blocking collectives: 224 us -> 0 us
  local copies, waits for them, and re-layouts: 96 us -> 1.33 us
  waiting for transfers between devices: 0 us -> 70.2 us
  Pallas kernels: 0 us -> 54.1 us
  matrix products: 46.4 us -> 0 us
  starting transfers between devices: 0 us -> 23.6 us
  other arithmetic: 17.4 us -> 1.74 us
    all_to_all x4 -> x0, blocking collectives: 224 us -> none  [the longest x1 85.5 us: on_device(): lax.all_to_all(triple, 'mem', split_axis=2, concat_axis=0, tiled=True)]
    all_to_all x0 -> x2, waiting for transfers between devices: none -> 58.7 us  [the longest x1 29.6 us: on_device(): lax.all_to_all(done.reshape(128, 8, D), ('mem', 'grp'), split_axis=0, con...]
    pallas_call x0 -> x5, Pallas kernels: none -> 54.1 us  [the longest x2 24.4 us: time_block(): pl.pallas_call(time_kernel, grid=(1,), in_specs=[pl.BlockSpec((GROUP, GRO...]
    reshape x7 -> x0, local copies, waits for them, and re-layouts: 52.1 us -> none  [the longest x2 31.9 us: attend_local(): pieces = triple.reshape(lead + (3, HEADS, HEAD))]
    dot_general x8 -> x0, matrix products: 46.4 us -> none  [the longest x2 19.3 us: make_triple(): jnp.dot(normed.reshape(-1, width), weight_in, preferred_element_type=jnp....]
    unnamed x13 -> x2, local copies, waits for them, and re-layouts: 19.6 us -> 1.33 us
    all_to_all x0 -> x2, starting transfers between devices: none -> 17.9 us  [the longest x1 11.3 us: on_device(): lax.all_to_all(to_columns(video), 'mem', split_axis=0, concat_axis=0, til...]
    slice x2 -> x0, local copies, waits for them, and re-layouts: 17.5 us -> none  [attend_local(): values = pieces[..., 2, :, :]]
  transfers between devices with their start and end apart: 0 -> 8, of which waited for: 0 -> 4; matrix products, arithmetic and copies ran while one was open for 0% -> 1% of each run, Pallas kernels for 0% -> 8%
where the time goes in v1:
time: 151 us
  waiting for transfers between devices  70.2 us (46%)
  Pallas kernels  54.1 us (36%)
  starting transfers between devices  23.6 us (16%)
  other arithmetic  1.74 us (1%)
    all_to_all x1, waiting for transfers between devices, on_device(): lax.all_to_all(done.reshape(128, 8, D), ('mem', 'grp'), split_axis=0, con...  29.6 us
    all_to_all x1, waiting for transfers between devices, on_device(): lax.all_to_all(to_columns(video), 'mem', split_axis=0, concat_axis=0, til...  29.1 us
    pallas_call x2, Pallas kernels, time_block(): pl.pallas_call(time_kernel, grid=(1,), in_specs=[pl.BlockSpec((GROUP, GRO...  24.4 us
    pallas_call x1, Pallas kernels, height_block(): pl.pallas_call(functools.partial(height_kernel, len(pieces)), grid=(1,),...  21 us
    ppermute x6, waiting for transfers between devices, on_device(): pieces.append(lax.ppermute(outs[s], 'grp', [(i, i ^ s) for i in range(4)]))  11.5 us
    all_to_all x1, starting transfers between devices, on_device(): lax.all_to_all(to_columns(video), 'mem', split_axis=0, concat_axis=0, til...  11.3 us
    all_to_all x1, starting transfers between devices, on_device(): lax.all_to_all(done.reshape(128, 8, D), ('mem', 'grp'), split_axis=0, con...  6.55 us
    ppermute x6, starting transfers between devices, on_device(): pieces.append(lax.ppermute(outs[s], 'grp', [(i, i ^ s) for i in range(4)]))  5.66 us
  transfers between devices with their start and end apart: 8, of which 4 were waited for; matrix products, arithmetic and copies ran while one was open for 1% of the time, Pallas kernels for 8%

profile of v1, /device:TPU:1, one launch (start us, length us, event | category | flops | bytes accessed | tf_op | source)
XLA Modules:
  0.0 151.0 jit_solution(16152981921915056642)
XLA Ops:
  0.0 0.8 fusion.3.perm_ref
  0.8 4.3 %to_columns.1 = bf16[32,4,8,1024]{3,2,1,0:T(8,128)(2,1)} custom-call(bf16[256,256]{1,0:T(8,128)(2,1)} %fusion.3.perm_ref, bf16[4,8,32,1024]{3,2,1,0:T(8,128)(2,1)} %x_ref.1), custom_call_target="tpu_custom_call" | custom-call | tf_op jit(solution)/shard_map/to_columns/pallas_call | solution.py:38
  5.1 11.3 %all-to-all-start = ((bf16[32,4,8,1024]{3,2,1,0:T(8,128)(2,1)}), bf16[32,4,8,1024]{3,2,1,0:T(8,128)(2,1)S(1)}, u32[]{:S(2)}, u32[]{:S(2)}) async-start(bf16[32,4,8,1024]{3,2,1,0:T(8,128)(2,1)} %to_columns.1), calls=%async_computation | async-start | bytes 4194304 | tf_op jit(solution)/shard_map/all_to_all | solution.py:231
  16.5 0.1 fusion.2.perm_ref
  16.6 29.1 %all-to-all-done.x_ref = bf16[32,4,8,1024]{3,2,1,0:T(8,128)(2,1)S(1)} async-done(((bf16[32,4,8,1024]{3,2,1,0:T(8,128)(2,1)}), bf16[32,4,8,1024]{3,2,1,0:T(8,128)(2,1)S(1)}, u32[]{:S(2)}, u32[]{:S(2)}) %all-to-all-start) | async-done | bytes 2097184 | tf_op jit(solution)/shard_map/all_to_all | solution.py:231
  45.6 12.2 %time_block_0.1 = (bf16[4,32,1024]{2,1,0:T(8,128)(2,1)S(1)}, bf16[4,32,1024]{2,1,0:T(8,128)(2,1)S(1)}, bf16[4,32,1024]{2,1,0:T(8,128)(2,1)S(1)}, bf16[4,32,1024]{2,1,0:T(8,128)(2,1)S(1)}) custom-call(bf16[256,256]{1,0:T(8,128)(2,1)S(1)} %fusion.2.perm_ref, bf16[32,4,8,1024]{3,2,1,0:T(8,128)(2,1)S(1)} %all-to-all-done.x_ref, bf16[2,1024,3072]{2,1,0:T(8,128)(2,1)} %refs_8_.1, ...), custom_call_target="tpu_custom_call" | custom-call | flops 4563402752 | bytes 10485760 | tf_op jit(solution)/shard_map/time_block_0/pallas_call | solution.py:159
  57.9 1.7 %collective-permute-start = (bf16[4,32,1024]{2,1,0:T(8,128)(2,1)S(1)}, bf16[4,32,1024]{2,1,0:T(8,128)(2,1)S(1)}, u32[]{:S(2)}, u32[]{:S(2)}) collective-permute-start(bf16[4,32,1024]{2,1,0:T(8,128)(2,1)S(1)} %get-tuple-element.14), channel_id=1, source_target_pairs={{0,32},{32,0},{64,96},{96,64},{1,33},{33,1},{65,97},{97,65},{2,34}... | collective-permute-start | bytes 786440 | tf_op jit(solution)/shard_map/ppermute | solution.py:237
  59.6 1.3 collective-permute-start.1
  60.9 0.4 collective-permute-start.2
  61.3 12.2 %time_block_1.1 = (bf16[4,32,1024]{2,1,0:T(8,128)(2,1)S(1)}, bf16[4,32,1024]{2,1,0:T(8,128)(2,1)S(1)}, bf16[4,32,1024]{2,1,0:T(8,128)(2,1)S(1)}, bf16[4,32,1024]{2,1,0:T(8,128)(2,1)S(1)}) custom-call(bf16[256,256]{1,0:T(8,128)(2,1)S(1)} %fusion.2.perm_ref, bf16[32,4,8,1024]{3,2,1,0:T(8,128)(2,1)S(1)} %all-to-all-done.x_ref, bf16[2,1024,3072]{2,1,0:T(8,128)(2,1)} %refs_8_.1, ...), custom_call_target="tpu_custom_call" | custom-call | flops 4563402752 | bytes 10485760 | tf_op jit(solution)/shard_map/time_block_1/pallas_call | solution.py:159
  73.5 0.2 collective-permute-start.3
  73.7 1.3 collective-permute-start.4
  75.0 0.0 collective-permute-done.refs_1_
  75.0 0.7 collective-permute-start.5
  75.8 0.1 fusion.1.perm_ref
  75.9 0.0 collective-permute-done.1.refs_2_
  75.9 0.0 collective-permute-done.2.refs_3_
  75.9 0.0 collective-permute-done.3.refs_5_
  75.9 5.4 %collective-permute-done.4.refs_6_ = bf16[4,32,1024]{2,1,0:T(8,128)(2,1)S(1)} collective-permute-done((bf16[4,32,1024]{2,1,0:T(8,128)(2,1)S(1)}, bf16[4,32,1024]{2,1,0:T(8,128)(2,1)S(1)}, u32[]{:S(2)}, u32[]{:S(2)}) %collective-permute-start.4) | collective-permute-done | bytes 262176 | tf_op jit(solution)/shard_map/ppermute | solution.py:237
  81.3 6.1 %collective-permute-done.5.refs_7_ = bf16[4,32,1024]{2,1,0:T(8,128)(2,1)S(1)} collective-permute-done((bf16[4,32,1024]{2,1,0:T(8,128)(2,1)S(1)}, bf16[4,32,1024]{2,1,0:T(8,128)(2,1)S(1)}, u32[]{:S(2)}, u32[]{:S(2)}) %collective-permute-start.5) | collective-permute-done | bytes 262176 | tf_op jit(solution)/shard_map/ppermute | solution.py:237
  87.4 21.0 %height_block_0.1 = bf16[32,32,1024]{2,1,0:T(8,128)(2,1)} custom-call(bf16[256,256]{1,0:T(8,128)(2,1)S(1)} %fusion.1.perm_ref, bf16[4,32,1024]{2,1,0:T(8,128)(2,1)S(1)} %get-tuple-element.13.refs_0_, bf16[4,32,1024]{2,1,0:T(8,128)(2,1)S(1)} %collective-permute-done.refs_1_, bf16[4,32,1024]{2,1,0:T(8,128)(2,1)S(1)} %collective-permute-done.1.refs_2_, ...), custom_call_target="tpu_custom_call" | custom-call | flops 9126805504 | bytes 12582912 | tf_op jit(solution)/shard_map/height_block_0/pallas_call | solution.py:199
  108.4 6.6 %all-to-all-start.1 = ((bf16[128,8,1024]{2,1,0:T(8,128)(2,1)}), bf16[128,8,1024]{2,1,0:T(8,128)(2,1)S(1)}, u32[]{:S(2)}, u32[]{:S(2)}) async-start(bf16[128,8,1024]{2,1,0:T(8,128)(2,1)} %bitcast), calls=%async_computation.1 | async-start | bytes 4194304 | tf_op jit(solution)/shard_map/all_to_all | solution.py:242
  114.9 0.7 fusion.perm_ref
  115.7 29.6 %all-to-all-done.1 = bf16[128,8,1024]{2,1,0:T(8,128)(2,1)S(1)} async-done(((bf16[128,8,1024]{2,1,0:T(8,128)(2,1)}), bf16[128,8,1024]{2,1,0:T(8,128)(2,1)S(1)}, u32[]{:S(2)}, u32[]{:S(2)}) %all-to-all-start.1) | async-done | bytes 2097184 | tf_op jit(solution)/shard_map/all_to_all | solution.py:242
  145.3 0.0 copy-start
  145.3 1.3 copy-done
  146.7 4.3 %to_tokens.1 = bf16[4,8,32,1024]{3,2,1,0:T(8,128)(2,1)} custom-call(bf16[256,256]{1,0:T(8,128)(2,1)} %fusion.perm_ref, bf16[32,4,8,1024]{3,2,1,0:T(8,128)(2,1)} %bitcast.2), custom_call_target="tpu_custom_call" | custom-call | tf_op jit(solution)/shard_map/to_tokens/pallas_call | solution.py:55
  (4 shorter events, 0.0 us)
Async XLA Ops:
  5.1 40.5 %all-to-all-start = ((bf16[32,4,8,1024]{3,2,1,0:T(8,128)(2,1)}), bf16[32,4,8,1024]{3,2,1,0:T(8,128)(2,1)S(1)}, u32[]{:S(2)}, u32[]{:S(2)}) async-start(bf16[32,4,8,1024]{3,2,1,0:T(8,128)(2,1)} %to_columns.1), calls=%async_computation | async-start | bytes 4194304 | tf_op jit(solution)/shard_map/all_to_all | solution.py:231
  57.9 17.2 %collective-permute-start = (bf16[4,32,1024]{2,1,0:T(8,128)(2,1)S(1)}, bf16[4,32,1024]{2,1,0:T(8,128)(2,1)S(1)}, u32[]{:S(2)}, u32[]{:S(2)}) collective-permute-start(bf16[4,32,1024]{2,1,0:T(8,128)(2,1)S(1)} %get-tuple-element.14), channel_id=1, source_target_pairs={{0,32},{32,0},{64,96},{96,64},{1,33},{33,1},{65,97},{97,65},{2,34}... | collective-permute-start | bytes 786440 | tf_op jit(solution)/shard_map/ppermute | solution.py:237
  59.6 16.3 %collective-permute-start.1 = (bf16[4,32,1024]{2,1,0:T(8,128)(2,1)S(1)}, bf16[4,32,1024]{2,1,0:T(8,128)(2,1)S(1)}, u32[]{:S(2)}, u32[]{:S(2)}) collective-permute-start(bf16[4,32,1024]{2,1,0:T(8,128)(2,1)S(1)} %get-tuple-element.15), channel_id=1, source_target_pairs={{0,64},{32,96},{64,0},{96,32},{1,65},{33,97},{65,1},{97,33},{2,66}... | collective-permute-start | bytes 786440 | tf_op jit(solution)/shard_map/ppermute | solution.py:237
  60.9 15.0 %collective-permute-start.2 = (bf16[4,32,1024]{2,1,0:T(8,128)(2,1)S(1)}, bf16[4,32,1024]{2,1,0:T(8,128)(2,1)S(1)}, u32[]{:S(2)}, u32[]{:S(2)}) collective-permute-start(bf16[4,32,1024]{2,1,0:T(8,128)(2,1)S(1)} %get-tuple-element.16), channel_id=1, source_target_pairs={{0,96},{32,64},{64,32},{96,0},{1,97},{33,65},{65,33},{97,1},{2,98}... | collective-permute-start | bytes 786440 | tf_op jit(solution)/shard_map/ppermute | solution.py:237
  73.5 2.4 %collective-permute-start.3 = (bf16[4,32,1024]{2,1,0:T(8,128)(2,1)S(1)}, bf16[4,32,1024]{2,1,0:T(8,128)(2,1)S(1)}, u32[]{:S(2)}, u32[]{:S(2)}) collective-permute-start(bf16[4,32,1024]{2,1,0:T(8,128)(2,1)S(1)} %get-tuple-element.18), channel_id=1, source_target_pairs={{0,32},{32,0},{64,96},{96,64},{1,33},{33,1},{65,97},{97,65},{2,34}... | collective-permute-start | bytes 786440 | tf_op jit(solution)/shard_map/ppermute | solution.py:237
  73.7 7.5 %collective-permute-start.4 = (bf16[4,32,1024]{2,1,0:T(8,128)(2,1)S(1)}, bf16[4,32,1024]{2,1,0:T(8,128)(2,1)S(1)}, u32[]{:S(2)}, u32[]{:S(2)}) collective-permute-start(bf16[4,32,1024]{2,1,0:T(8,128)(2,1)S(1)} %get-tuple-element.19), channel_id=1, source_target_pairs={{0,64},{32,96},{64,0},{96,32},{1,65},{33,97},{65,1},{97,33},{2,66}... | collective-permute-start | bytes 786440 | tf_op jit(solution)/shard_map/ppermute | solution.py:237
  75.0 12.4 %collective-permute-start.5 = (bf16[4,32,1024]{2,1,0:T(8,128)(2,1)S(1)}, bf16[4,32,1024]{2,1,0:T(8,128)(2,1)S(1)}, u32[]{:S(2)}, u32[]{:S(2)}) collective-permute-start(bf16[4,32,1024]{2,1,0:T(8,128)(2,1)S(1)} %get-tuple-element.20), channel_id=1, source_target_pairs={{0,96},{32,64},{64,32},{96,0},{1,97},{33,65},{65,33},{97,1},{2,98}... | collective-permute-start | bytes 786440 | tf_op jit(solution)/shard_map/ppermute | solution.py:237
  108.4 37.0 %all-to-all-start.1 = ((bf16[128,8,1024]{2,1,0:T(8,128)(2,1)}), bf16[128,8,1024]{2,1,0:T(8,128)(2,1)S(1)}, u32[]{:S(2)}, u32[]{:S(2)}) async-start(bf16[128,8,1024]{2,1,0:T(8,128)(2,1)} %bitcast), calls=%async_computation.1 | async-start | bytes 4194304 | tf_op jit(solution)/shard_map/all_to_all | solution.py:242
  145.3 1.3 copy-start

commit v2 on v1

v2 whole, which is shorter than its diff:
```python
import functools
import math

import jax
import jax.numpy as jnp
from jax import lax
from jax.experimental import pallas as pl
from jax.experimental.pallas import tpu as pltpu
from jax.sharding import PartitionSpec as P

D = 1024
HEADS = 16
HEAD = 64
EPS = 1e-06
PAIRS = HEADS // 2
SCALE = math.log2(math.e) / math.sqrt(HEAD)
BF = jnp.bfloat16
F32 = jnp.float32

LINE = 128
GROUP = 256
LIMIT = 50 * 2**20
STEP = 512


def permutation(rows, columns):
    return (rows[:, None] == columns[None, :]).astype(BF)


def reorder(source, x):
    row = lax.broadcasted_iota(jnp.int32, (GROUP, GROUP), 0)
    column = lax.broadcasted_iota(jnp.int32, (GROUP, GROUP), 1)
    perm = (source(row) == column).astype(F32).astype(BF)
    return jnp.dot(perm, x, preferred_element_type=F32).astype(BF)


def to_columns_kernel(x_ref, o_ref, held_ref, sems):
    copies = [
        pltpu.make_async_copy(x_ref.at[:, pl.ds(2 * t, 2)], held_ref.at[t], sems.at[t])
        for t in range(4)
    ]
    for copy in copies:
        copy.start()
    for t, copy in enumerate(copies):
        copy.wait()
        y = reorder(
            lambda o: (o % 4) * 64 + ((o // 4) % 2) * 32 + o // 8, held_ref[t].reshape(GROUP, D)
        )
        o_ref[:, t] = y.reshape(32, 8, D)


def to_columns(video):
    return pl.pallas_call(
        to_columns_kernel,
        in_specs=[pl.BlockSpec(memory_space=pltpu.HBM)],
        out_specs=pl.BlockSpec(memory_space=pltpu.VMEM),
        out_shape=jax.ShapeDtypeStruct((32, 4, 8, D), BF),
        scratch_shapes=[pltpu.VMEM((4, 4, 2, 32, D), BF), pltpu.SemaphoreType.DMA((4,))],
        compiler_params=pltpu.CompilerParams(vmem_limit_bytes=60 * 2**20),
        name="to_columns",
    )(video)


def to_tokens_kernel(x_ref, o_ref, held_ref, sems):
    copies = []
    for j in range(4):
        y = reorder(lambda o: (o % 32) * 8 + o // 32, x_ref[:, j].reshape(GROUP, D))
        held_ref[j] = y.reshape(8, 32, D)
        copies.append(pltpu.make_async_copy(held_ref.at[j], o_ref.at[j], sems.at[j]))
        copies[-1].start()
    for copy in copies:
        copy.wait()


def to_tokens(columns):
    return pl.pallas_call(
        to_tokens_kernel,
        in_specs=[pl.BlockSpec(memory_space=pltpu.VMEM)],
        out_specs=pl.BlockSpec(memory_space=pltpu.HBM),
        out_shape=jax.ShapeDtypeStruct((4, 8, 32, D), BF),
        scratch_shapes=[pltpu.VMEM((4, 8, 32, D), BF), pltpu.SemaphoreType.DMA((4,))],
        compiler_params=pltpu.CompilerParams(vmem_limit_bytes=LIMIT),
        name="to_tokens",
    )(columns)


def weight_copies(w_ref, wo_ref, w_held, wo_held, sems, layer):
    copies = [
        pltpu.make_async_copy(
            w_ref.at[layer, :, pl.ds(i * STEP, STEP)],
            w_held.at[:, pl.ds(i * STEP, STEP)],
            sems.at[i],
        )
        for i in range(3 * D // STEP)
    ]
    copies.append(pltpu.make_async_copy(wo_ref.at[layer], wo_held, sems.at[3 * D // STEP]))
    return copies


def load_tokens(perm, pieces, xp_ref, normed_ref, at):
    x = jnp.concatenate(pieces, axis=0) if len(pieces) > 1 else pieces[0]
    x = jnp.dot(perm, x, preferred_element_type=F32)
    xp_ref[pl.ds(at, GROUP), :] = x.astype(BF)
    power = jnp.mean(x * x, axis=-1, keepdims=True)
    normed_ref[pl.ds(at, GROUP), :] = (x * lax.rsqrt(power + EPS)).astype(BF)


def project(normed_ref, w_ref, qkv_ref, copies):
    for i, copy in enumerate(copies):
        copy.wait()
        at = i * STEP
        acc = jnp.dot(normed_ref[...], w_ref[:, at : at + STEP], preferred_element_type=F32)
        qkv_ref[:, at : at + STEP] = acc.astype(BF)


def attend(qkv_ref, ctx_ref, masked):
    tokens = qkv_ref.shape[0]
    low = (lax.broadcasted_iota(jnp.int32, (LINE, LINE), 1) < HEAD).astype(F32)
    low, high = low.astype(BF), (1.0 - low).astype(BF)
    if masked:
        a = lax.broadcasted_iota(jnp.int32, (2 * LINE, LINE), 0) % LINE // 32
        b = lax.broadcasted_iota(jnp.int32, (2 * LINE, LINE), 1) // 32
        same = a == b

    @pl.loop(0, tokens // LINE)
    def _(i):
        rows = pl.ds(pl.multiple_of(i * LINE, LINE), LINE)
        for p in range(PAIRS):
            q = qkv_ref[rows, p * 128 : p * 128 + 128]
            k = qkv_ref[rows, D + p * 128 : D + p * 128 + 128]
            v = qkv_ref[rows, 2 * D + p * 128 : 2 * D + p * 128 + 128]
            q = jnp.concatenate([q * low, q * high], axis=0)
            s = lax.dot_general(q, k, (((1,), (1,)), ((), ())), preferred_element_type=F32)
            if masked:
                s = jnp.where(same, s, -1e30)
            top = jnp.max(s, axis=-1, keepdims=True)
            e = jnp.exp2((s - top) * SCALE).astype(BF)
            e = jnp.concatenate([e[:LINE], e[LINE:]], axis=1)
            v = jnp.concatenate(
                [
                    jnp.concatenate([v * low, low], axis=1),
                    jnp.concatenate([v * high, high], axis=1),
                ],
                axis=0,
            )
            o = jnp.dot(e, v, preferred_element_type=F32)
            ctx_ref[rows, p * 128 : p * 128 + 128] = (o[:, :128] / o[:, 128:]).astype(BF)


def update(xp_ref, ctx_ref, wo_ref, y_ref, step=512):
    for at in range(0, D, step):
        acc = jnp.dot(ctx_ref[...], wo_ref[:, at : at + step], preferred_element_type=F32)
        y_ref[:, at : at + step] = (xp_ref[:, at : at + step].astype(F32) + acc).astype(BF)


def run_block(loads, w_refs, work, layer, masked):
    w_ref, wo_ref = w_refs
    xp_ref, normed_ref, qkv_ref, ctx_ref, w_held, wo_held, sems = work
    copies = weight_copies(w_ref, wo_ref, w_held, wo_held, sems, layer)
    for copy in copies:
        copy.start()
    loads(xp_ref, normed_ref)
    project(normed_ref, w_held, qkv_ref, copies[:-1])
    attend(qkv_ref, ctx_ref, masked)
    copies[-1].wait()
    update(xp_ref, ctx_ref, wo_held, normed_ref)
    return normed_ref


def scratch(tokens):
    return [
        pltpu.VMEM((tokens, D), BF),
        pltpu.VMEM((tokens, D), BF),
        pltpu.VMEM((tokens, 3 * D), BF),
        pltpu.VMEM((tokens, D), BF),
        pltpu.VMEM((D, 3 * D), BF),
        pltpu.VMEM((D, D), BF),
        pltpu.SemaphoreType.DMA((3 * D // STEP + 1,)),
    ]


def block_cost(tokens):
    return pl.CostEstimate(
        flops=2 * tokens * D * D * 4 + 4 * tokens * 128 * D,
        bytes_accessed=8 * D * D + 4 * tokens * D,
        transcendentals=tokens * 128 * HEADS,
    )


def time_kernel(perm_ref, x_ref, *refs, k, groups, halves):
    w_refs, outs, work = refs[:2], refs[2 : 2 + 4 * halves], refs[2 + 4 * halves :]

    def loads(xp_ref, normed_ref):
        perm = perm_ref[...]
        for t in range(groups):
            x = x_ref[:, k * groups + t].reshape(GROUP, D)
            load_tokens(perm, [x], xp_ref, normed_ref, t * GROUP)

    y_ref = run_block(loads, w_refs, work, 0, False)
    span = 32 // halves
    for r in range(2 * groups):
        for s in range(4):
            for h in range(halves):
                at = (r * 4 + s) * 32 + h * span
                outs[s * halves + h][r] = y_ref[at : at + span, :]


def time_block(perm, lines, w_triple, w_out, k, groups, halves):
    tokens = groups * GROUP
    return pl.pallas_call(
        functools.partial(time_kernel, k=k, groups=groups, halves=halves),
        in_specs=[pl.BlockSpec(memory_space=pltpu.VMEM)] * 2
        + [pl.BlockSpec(memory_space=pltpu.HBM)] * 2,
        out_specs=[pl.BlockSpec(memory_space=pltpu.VMEM)] * (4 * halves),
        out_shape=[jax.ShapeDtypeStruct((2 * groups, 32 // halves, D), BF)] * (4 * halves),
        scratch_shapes=scratch(tokens),
        cost_estimate=block_cost(tokens),
        compiler_params=pltpu.CompilerParams(vmem_limit_bytes=LIMIT),
        name=f"time_block_{k}",
    )(perm, lines, w_triple, w_out)


def height_kernel(perm_ref, *refs, offsets, groups):
    n = len(offsets)
    pieces, w_refs, y_ref, work = refs[:n], refs[n : n + 2], refs[n + 2], refs[n + 3 :]

    def loads(xp_ref, normed_ref):
        perm = perm_ref[...]
        for t in range(groups):
            parts = [
                piece[r, at + t * 8 : at + t * 8 + 8, :]
                for piece, at in zip(pieces, offsets)
                for r in range(piece.shape[0])
            ]
            load_tokens(perm, parts, xp_ref, normed_ref, t * GROUP)

    out = run_block(loads, w_refs, work, 1, True)
    y_ref[...] = out[...].reshape(y_ref.shape)


def height_block(perm, pieces, offsets, w_triple, w_out, k, groups):
    tokens = groups * GROUP
    return pl.pallas_call(
        functools.partial(height_kernel, offsets=offsets, groups=groups),
        in_specs=[pl.BlockSpec(memory_space=pltpu.VMEM)] * (len(pieces) + 1)
        + [pl.BlockSpec(memory_space=pltpu.HBM)] * 2,
        out_specs=pl.BlockSpec(memory_space=pltpu.VMEM),
        out_shape=jax.ShapeDtypeStruct((8 * groups, 32, D), BF),
        scratch_shapes=scratch(tokens),
        cost_estimate=block_cost(tokens),
        compiler_params=pltpu.CompilerParams(vmem_limit_bytes=LIMIT),
        name=f"height_block_{k}",
    )(perm, *pieces, w_triple, w_out)


CHUNKS0 = 2
CHUNKS1 = 1
HALVES = (1, 1)


def on_device(video, w_triple, w_out):
    g = lax.axis_index("grp")
    o = jnp.arange(GROUP)
    want = (o % 32) * 8 + (o // 128) * 4 + (((o // 32) % 4) ^ g)
    perm0 = permutation(want, o)
    rows = 8 // CHUNKS0
    m, rg, r = o // 32, (o // 8) % 4, o % 8
    want = (((r // rows) * 4 + (rg ^ g)) * rows + r % rows) * 8 + m
    perm1 = permutation(want, o)

    lines = lax.all_to_all(to_columns(video), "mem", split_axis=0, concat_axis=0, tiled=True)
    pieces = []
    for k in range(CHUNKS0):
        halves = HALVES[k]
        outs = time_block(perm0, lines, w_triple, w_out, k, 4 // CHUNKS0, halves)
        for s in range(4):
            pairs = [(i, i ^ s) for i in range(4)]
            trade = (lambda x: lax.ppermute(x, "grp", pairs)) if s else (lambda x: x)
            pieces.append([trade(outs[s * halves + h]) for h in range(halves)])
    done = []
    for k in range(CHUNKS1):
        at = k * 32 // CHUNKS1
        chosen, offsets = [], []
        for piece in pieces:
            span = piece[0].shape[1]
            chosen.append(piece[at // span])
            offsets.append(at % span)
        done.append(
            height_block(perm1, chosen, tuple(offsets), w_triple, w_out, k, 4 // CHUNKS1)
        )
    done = jnp.concatenate(done, axis=0) if CHUNKS1 > 1 else done[0]
    done = lax.all_to_all(
        done.reshape(128, 8, D), ("mem", "grp"), split_axis=0, concat_axis=0, tiled=True
    )
    return to_tokens(done.reshape(32, 4, 8, D))


def solution(mesh):
    return jax.shard_map(
        on_device,
        mesh=mesh,
        in_specs=(P("mem", "grp", None, None), P(), P()),
        out_specs=P("mem", "grp", None, None),
        check_vma=False,
    )
```

time: 151 us -> 139 us (0.921)
  blocking collectives: 0 us -> 37 us
  waiting for transfers between devices: 70.2 us -> 40.6 us
  Pallas kernels: 54.1 us -> 43.4 us
  starting transfers between devices: 23.6 us -> 17 us
  other arithmetic: 1.74 us -> 0.22 us
    all_to_all x0 -> x1, blocking collectives: none -> 37 us  [on_device(): lax.all_to_all(done.reshape(128, 8, D), ('mem', 'grp'), split_axis=0, con...]
    all_to_all x1 -> x0, waiting for transfers between devices: 29.6 us -> none  [on_device(): lax.all_to_all(done.reshape(128, 8, D), ('mem', 'grp'), split_axis=0, con...]
    pallas_call x5, Pallas kernels: 54.1 us -> 43.4 us  [the longest x2 19.5 us: time_block(): pl.pallas_call(functools.partial(time_kernel, k=k, groups=groups, halves=...]
    all_to_all x1 -> x0, starting transfers between devices: 6.55 us -> none  [on_device(): lax.all_to_all(done.reshape(128, 8, D), ('mem', 'grp'), split_axis=0, con...]
  transfers between devices with their start and end apart: 8 -> 7, of which waited for: 4 -> 3; matrix products, arithmetic and copies ran while one was open for 1% -> 0% of each run, Pallas kernels for 8% -> 7%
where the time goes in v2:
time: 139 us; the launch traced here: 138 us
  Pallas kernels  43.4 us (31%)
  waiting for transfers between devices  40.6 us (29%)
  blocking collectives  37 us (27%)
  starting transfers between devices  17 us (12%)
    all_to_all x1, blocking collectives, on_device(): lax.all_to_all(done.reshape(128, 8, D), ('mem', 'grp'), split_axis=0, con...  37 us
    all_to_all x1, waiting for transfers between devices, on_device(): lax.all_to_all(to_columns(video), 'mem', split_axis=0, concat_axis=0, til...  29.1 us
    pallas_call x2, Pallas kernels, time_block(): pl.pallas_call(functools.partial(time_kernel, k=k, groups=groups, halves=...  19.5 us
    pallas_call x1, Pallas kernels, height_block(): pl.pallas_call(functools.partial(height_kernel, offsets=offsets, groups=g...  18.6 us
    ppermute x6, waiting for transfers between devices, on_device(): trade = (lambda x: lax.ppermute(x, 'grp', pairs)) if s else lambda x: x  11.5 us
    all_to_all x1, starting transfers between devices, on_device(): lax.all_to_all(to_columns(video), 'mem', split_axis=0, concat_axis=0, til...  11.4 us
    ppermute x6, starting transfers between devices, on_device(): trade = (lambda x: lax.ppermute(x, 'grp', pairs)) if s else lambda x: x  5.66 us
    pallas_call x1, Pallas kernels, to_columns(): pl.pallas_call(to_columns_kernel, in_specs=[pl.BlockSpec(memory_space=plt...  3.61 us
  transfers between devices with their start and end apart: 7, of which 3 were waited for; matrix products, arithmetic and copies ran while one was open for 0% of the time, Pallas kernels for 7%

profile of v2, /device:TPU:1, one launch (start us, length us, event | category | flops | bytes accessed | tf_op | source)
XLA Modules:
  0.0 138.4 jit_solution(14357514222522220989)
XLA Ops:
  0.0 3.6 %to_columns.1 = bf16[32,4,8,1024]{3,2,1,0:T(8,128)(2,1)} custom-call(bf16[4,8,32,1024]{3,2,1,0:T(8,128)(2,1)} %x_ref.1), custom_call_target="tpu_custom_call" | custom-call | tf_op jit(solution)/shard_map/to_columns/pallas_call | solution.py:53
  3.6 11.4 %all-to-all-start = ((bf16[32,4,8,1024]{3,2,1,0:T(8,128)(2,1)}), bf16[32,4,8,1024]{3,2,1,0:T(8,128)(2,1)S(1)}, u32[]{:S(2)}, u32[]{:S(2)}) async-start(bf16[32,4,8,1024]{3,2,1,0:T(8,128)(2,1)} %to_columns.1), calls=%async_computation | async-start | bytes 4194304 | tf_op jit(solution)/shard_map/all_to_all | solution.py:271
  15.0 0.1 fusion.1.perm_ref
  15.1 29.1 %all-to-all-done.x_ref = bf16[32,4,8,1024]{3,2,1,0:T(8,128)(2,1)S(1)} async-done(((bf16[32,4,8,1024]{3,2,1,0:T(8,128)(2,1)}), bf16[32,4,8,1024]{3,2,1,0:T(8,128)(2,1)S(1)}, u32[]{:S(2)}, u32[]{:S(2)}) %all-to-all-start) | async-done | bytes 2097184 | tf_op jit(solution)/shard_map/all_to_all | solution.py:271
  44.2 9.8 %time_block_0.1 = (bf16[4,32,1024]{2,1,0:T(8,128)(2,1)S(1)}, bf16[4,32,1024]{2,1,0:T(8,128)(2,1)S(1)}, bf16[4,32,1024]{2,1,0:T(8,128)(2,1)S(1)}, bf16[4,32,1024]{2,1,0:T(8,128)(2,1)S(1)}) custom-call(bf16[256,256]{1,0:T(8,128)(2,1)S(1)} %fusion.1.perm_ref, bf16[32,4,8,1024]{3,2,1,0:T(8,128)(2,1)S(1)} %all-to-all-done.x_ref, bf16[2,1024,3072]{2,1,0:T(8,128)(2,1)} %refs_8_.1, ...), custom_call_target="tpu_custom_call" | custom-call | flops 4563402752 | bytes 10485760 | tf_op jit(solution)/shard_map/time_block_0/pallas_call | solution.py:210
  54.0 1.7 %collective-permute-start = (bf16[4,32,1024]{2,1,0:T(8,128)(2,1)S(1)}, bf16[4,32,1024]{2,1,0:T(8,128)(2,1)S(1)}, u32[]{:S(2)}, u32[]{:S(2)}) collective-permute-start(bf16[4,32,1024]{2,1,0:T(8,128)(2,1)S(1)} %get-tuple-element.14), channel_id=1, source_target_pairs={{0,32},{32,0},{64,96},{96,64},{1,33},{33,1},{65,97},{97,65},{2,34}... | collective-permute-start | bytes 786440 | tf_op jit(solution)/shard_map/ppermute | solution.py:278
  55.7 1.3 collective-permute-start.1
  56.9 0.5 collective-permute-start.2
  57.4 9.8 %time_block_1.1 = (bf16[4,32,1024]{2,1,0:T(8,128)(2,1)S(1)}, bf16[4,32,1024]{2,1,0:T(8,128)(2,1)S(1)}, bf16[4,32,1024]{2,1,0:T(8,128)(2,1)S(1)}, bf16[4,32,1024]{2,1,0:T(8,128)(2,1)S(1)}) custom-call(bf16[256,256]{1,0:T(8,128)(2,1)S(1)} %fusion.1.perm_ref, bf16[32,4,8,1024]{3,2,1,0:T(8,128)(2,1)S(1)} %all-to-all-done.x_ref, bf16[2,1024,3072]{2,1,0:T(8,128)(2,1)} %refs_8_.1, ...), custom_call_target="tpu_custom_call" | custom-call | flops 4563402752 | bytes 10485760 | tf_op jit(solution)/shard_map/time_block_1/pallas_call | solution.py:210
  67.2 0.2 collective-permute-start.3
  67.4 1.2 collective-permute-start.4
  68.7 0.0 collective-permute-done.refs_1_
  68.7 0.7 collective-permute-start.5
  69.4 0.1 fusion.perm_ref
  69.5 0.0 collective-permute-done.1.refs_2_
  69.5 0.0 collective-permute-done.2.refs_3_
  69.6 0.0 collective-permute-done.3.refs_5_
  69.6 5.4 %collective-permute-done.4.refs_6_ = bf16[4,32,1024]{2,1,0:T(8,128)(2,1)S(1)} collective-permute-done((bf16[4,32,1024]{2,1,0:T(8,128)(2,1)S(1)}, bf16[4,32,1024]{2,1,0:T(8,128)(2,1)S(1)}, u32[]{:S(2)}, u32[]{:S(2)}) %collective-permute-start.4) | collective-permute-done | bytes 262176 | tf_op jit(solution)/shard_map/ppermute | solution.py:278
  74.9 6.1 %collective-permute-done.5.refs_7_ = bf16[4,32,1024]{2,1,0:T(8,128)(2,1)S(1)} collective-permute-done((bf16[4,32,1024]{2,1,0:T(8,128)(2,1)S(1)}, bf16[4,32,1024]{2,1,0:T(8,128)(2,1)S(1)}, u32[]{:S(2)}, u32[]{:S(2)}) %collective-permute-start.5) | collective-permute-done | bytes 262176 | tf_op jit(solution)/shard_map/ppermute | solution.py:278
  81.1 18.6 %height_block_0.1 = bf16[32,32,1024]{2,1,0:T(8,128)(2,1)} custom-call(bf16[256,256]{1,0:T(8,128)(2,1)S(1)} %fusion.perm_ref, bf16[4,32,1024]{2,1,0:T(8,128)(2,1)S(1)} %get-tuple-element.13.refs_0_, bf16[4,32,1024]{2,1,0:T(8,128)(2,1)S(1)} %collective-permute-done.refs_1_, bf16[4,32,1024]{2,1,0:T(8,128)(2,1)S(1)} %collective-permute-done.1.refs_2_, ...), custom_call_target="tpu_custom_call" | custom-call | flops 9126805504 | bytes 12582912 | tf_op jit(solution)/shard_map/height_block_0/pallas_call | solution.py:243
  99.7 37.0 %all_to_all.10 = bf16[128,8,1024]{2,1,0:T(8,128)(2,1)S(1)} all-to-all(bf16[128,8,1024]{2,1,0:T(8,128)(2,1)} %bitcast.3), channel_id=1, replica_groups=mesh['grp'=4,'mem'=32] {'mem','grp'}, dimensions={0} | all-to-all | bytes 4194304 | tf_op jit(solution)/shard_map/all_to_all | solution.py:292
  136.6 1.6 %to_tokens.1 = bf16[4,8,32,1024]{3,2,1,0:T(8,128)(2,1)} custom-call(bf16[32,4,8,1024]{3,2,1,0:T(8,128)(2,1)S(1)} %bitcast.2), custom_call_target="tpu_custom_call" | custom-call | tf_op jit(solution)/shard_map/to_tokens/pallas_call | solution.py:76
  (2 shorter events, 0.0 us)
Async XLA Ops:
  3.6 40.6 %all-to-all-start = ((bf16[32,4,8,1024]{3,2,1,0:T(8,128)(2,1)}), bf16[32,4,8,1024]{3,2,1,0:T(8,128)(2,1)S(1)}, u32[]{:S(2)}, u32[]{:S(2)}) async-start(bf16[32,4,8,1024]{3,2,1,0:T(8,128)(2,1)} %to_columns.1), calls=%async_computation | async-start | bytes 4194304 | tf_op jit(solution)/shard_map/all_to_all | solution.py:271
  54.0 14.7 %collective-permute-start = (bf16[4,32,1024]{2,1,0:T(8,128)(2,1)S(1)}, bf16[4,32,1024]{2,1,0:T(8,128)(2,1)S(1)}, u32[]{:S(2)}, u32[]{:S(2)}) collective-permute-start(bf16[4,32,1024]{2,1,0:T(8,128)(2,1)S(1)} %get-tuple-element.14), channel_id=1, source_target_pairs={{0,32},{32,0},{64,96},{96,64},{1,33},{33,1},{65,97},{97,65},{2,34}... | collective-permute-start | bytes 786440 | tf_op jit(solution)/shard_map/ppermute | solution.py:278
  55.7 13.9 %collective-permute-start.1 = (bf16[4,32,1024]{2,1,0:T(8,128)(2,1)S(1)}, bf16[4,32,1024]{2,1,0:T(8,128)(2,1)S(1)}, u32[]{:S(2)}, u32[]{:S(2)}) collective-permute-start(bf16[4,32,1024]{2,1,0:T(8,128)(2,1)S(1)} %get-tuple-element.15), channel_id=1, source_target_pairs={{0,64},{32,96},{64,0},{96,32},{1,65},{33,97},{65,1},{97,33},{2,66}... | collective-permute-start | bytes 786440 | tf_op jit(solution)/shard_map/ppermute | solution.py:278
  56.9 12.6 %collective-permute-start.2 = (bf16[4,32,1024]{2,1,0:T(8,128)(2,1)S(1)}, bf16[4,32,1024]{2,1,0:T(8,128)(2,1)S(1)}, u32[]{:S(2)}, u32[]{:S(2)}) collective-permute-start(bf16[4,32,1024]{2,1,0:T(8,128)(2,1)S(1)} %get-tuple-element.16), channel_id=1, source_target_pairs={{0,96},{32,64},{64,32},{96,0},{1,97},{33,65},{65,33},{97,1},{2,98}... | collective-permute-start | bytes 786440 | tf_op jit(solution)/shard_map/ppermute | solution.py:278
  67.2 2.4 %collective-permute-start.3 = (bf16[4,32,1024]{2,1,0:T(8,128)(2,1)S(1)}, bf16[4,32,1024]{2,1,0:T(8,128)(2,1)S(1)}, u32[]{:S(2)}, u32[]{:S(2)}) collective-permute-start(bf16[4,32,1024]{2,1,0:T(8,128)(2,1)S(1)} %get-tuple-element.18), channel_id=1, source_target_pairs={{0,32},{32,0},{64,96},{96,64},{1,33},{33,1},{65,97},{97,65},{2,34}... | collective-permute-start | bytes 786440 | tf_op jit(solution)/shard_map/ppermute | solution.py:278
  67.4 7.5 %collective-permute-start.4 = (bf16[4,32,1024]{2,1,0:T(8,128)(2,1)S(1)}, bf16[4,32,1024]{2,1,0:T(8,128)(2,1)S(1)}, u32[]{:S(2)}, u32[]{:S(2)}) collective-permute-start(bf16[4,32,1024]{2,1,0:T(8,128)(2,1)S(1)} %get-tuple-element.19), channel_id=1, source_target_pairs={{0,64},{32,96},{64,0},{96,32},{1,65},{33,97},{65,1},{97,33},{2,66}... | collective-permute-start | bytes 786440 | tf_op jit(solution)/shard_map/ppermute | solution.py:278
  68.7 12.4 %collective-permute-start.5 = (bf16[4,32,1024]{2,1,0:T(8,128)(2,1)S(1)}, bf16[4,32,1024]{2,1,0:T(8,128)(2,1)S(1)}, u32[]{:S(2)}, u32[]{:S(2)}) collective-permute-start(bf16[4,32,1024]{2,1,0:T(8,128)(2,1)S(1)} %get-tuple-element.20), channel_id=1, source_target_pairs={{0,96},{32,64},{64,32},{96,0},{1,97},{33,65},{65,33},{97,1},{2,98}... | collective-permute-start | bytes 786440 | tf_op jit(solution)/shard_map/ppermute | solution.py:278

commit v3 on v0

v3 whole, which is shorter than its diff:
```python
import functools
import math

import jax
import jax.numpy as jnp
from jax import lax
from jax.experimental import pallas as pl
from jax.experimental.pallas import tpu as pltpu
from jax.sharding import PartitionSpec as P

D = 1024
HEADS = 16
HEAD = 64
EPS = 1e-06
PAIRS = HEADS // 2
SCALE = math.log2(math.e) / math.sqrt(HEAD)
BF = jnp.bfloat16
F32 = jnp.float32

LINE = 128
GROUP = 256
LIMIT = 50 * 2**20
STEP = 512


def permutation(rows, columns):
    return (rows[:, None] == columns[None, :]).astype(BF)


def reorder(source, x):
    row = lax.broadcasted_iota(jnp.int32, (GROUP, GROUP), 0)
    column = lax.broadcasted_iota(jnp.int32, (GROUP, GROUP), 1)
    perm = (source(row) == column).astype(F32).astype(BF)
    return jnp.dot(perm, x, preferred_element_type=F32).astype(BF)


def to_columns_kernel(x_ref, o_ref, held_ref, out_ref, sems, out_sems):
    copies = [
        pltpu.make_async_copy(x_ref.at[:, pl.ds(2 * t, 2)], held_ref.at[t], sems.at[t])
        for t in range(4)
    ]
    for copy in copies:
        copy.start()
    outs = []
    for t, copy in enumerate(copies):
        copy.wait()
        y = reorder(
            lambda o: (o % 4) * 64 + ((o // 4) % 2) * 32 + o // 8, held_ref[t].reshape(GROUP, D)
        )
        out_ref[t] = y.reshape(32, 8, D)
        outs.append(pltpu.make_async_copy(out_ref.at[t], o_ref.at[:, t], out_sems.at[t]))
        outs[-1].start()
    for copy in outs:
        copy.wait()


def to_columns(video):
    return pl.pallas_call(
        to_columns_kernel,
        in_specs=[pl.BlockSpec(memory_space=pltpu.HBM)],
        out_specs=pl.BlockSpec(memory_space=pltpu.HBM),
        out_shape=jax.ShapeDtypeStruct((32, 4, 8, D), BF),
        scratch_shapes=[
            pltpu.VMEM((4, 4, 2, 32, D), BF),
            pltpu.VMEM((4, 32, 8, D), BF),
            pltpu.SemaphoreType.DMA((4,)),
            pltpu.SemaphoreType.DMA((4,)),
        ],
        compiler_params=pltpu.CompilerParams(vmem_limit_bytes=60 * 2**20),
        name="to_columns",
    )(video)


def to_tokens_kernel(x_ref, o_ref, held_ref, sems):
    copies = []
    for j in range(4):
        y = reorder(lambda o: (o % 32) * 8 + o // 32, x_ref[:, j].reshape(GROUP, D))
        held_ref[j] = y.reshape(8, 32, D)
        copies.append(pltpu.make_async_copy(held_ref.at[j], o_ref.at[j], sems.at[j]))
        copies[-1].start()
    for copy in copies:
        copy.wait()


def to_tokens(columns):
    return pl.pallas_call(
        to_tokens_kernel,
        in_specs=[pl.BlockSpec(memory_space=pltpu.VMEM)],
        out_specs=pl.BlockSpec(memory_space=pltpu.HBM),
        out_shape=jax.ShapeDtypeStruct((4, 8, 32, D), BF),
        scratch_shapes=[pltpu.VMEM((4, 8, 32, D), BF), pltpu.SemaphoreType.DMA((4,))],
        compiler_params=pltpu.CompilerParams(vmem_limit_bytes=LIMIT),
        name="to_tokens",
    )(columns)


def weight_copy(w_ref, w_held, sems, layer, i):
    columns = pl.ds(pl.multiple_of(i * STEP, STEP), STEP)
    return pltpu.make_async_copy(
        w_ref.at[layer, :, columns], w_held.at[:, columns], sems.at[i]
    )


def load_tokens(perm, x, xp_ref, normed_ref, at):
    x = jnp.dot(perm, x, preferred_element_type=F32)
    rows = slice(at, at + x.shape[0])
    xp_ref[rows, :] = x.astype(BF)
    power = jnp.mean(x * x, axis=-1, keepdims=True)
    normed_ref[rows, :] = (x * lax.rsqrt(power + EPS)).astype(BF)


def project(normed_ref, w_held, qkv_ref, wait):
    for i in range(3 * D // STEP):
        wait(i)
        columns = slice(i * STEP, i * STEP + STEP)
        acc = jnp.dot(normed_ref[...], w_held[:, columns], preferred_element_type=F32)
        qkv_ref[:, columns] = acc.astype(BF)


def masks():
    low = (lax.broadcasted_iota(jnp.int32, (LINE, LINE), 1) < HEAD).astype(F32)
    return low.astype(BF), (1.0 - low).astype(BF)


def attend(q, k, v, low, high, same):
    q = jnp.concatenate([q * low, q * high], axis=0)
    s = lax.dot_general(q, k, (((1,), (1,)), ((), ())), preferred_element_type=F32)
    if same is not None:
        s = jnp.where(same, s, -1e30)
    top = jnp.max(s, axis=-1, keepdims=True)
    e = jnp.exp2((s - top) * SCALE).astype(BF)
    e = jnp.concatenate([e[:LINE], e[LINE:]], axis=1)
    v = jnp.concatenate(
        [
            jnp.concatenate([v * low, low], axis=1),
            jnp.concatenate([v * high, high], axis=1),
        ],
        axis=0,
    )
    o = jnp.dot(e, v, preferred_element_type=F32)
    return (o[:, :LINE] / o[:, LINE:]).astype(BF)


def start_weights(w_ref, w_held, sems, layer):
    copies = [weight_copy(w_ref, w_held, sems, layer, i) for i in range(3 * D // STEP)]
    for copy in copies:
        copy.start()
    return lambda i: copies[i].wait()


def cost(tokens, matmuls, attends):
    return pl.CostEstimate(
        flops=2 * tokens * D * D * matmuls + 4 * attends * 128 * D,
        bytes_accessed=2 * matmuls * D * D,
        transcendentals=attends * 128 * HEADS,
    )


def call(kernel, vmem, hbm, outs, scratch, estimate, name):
    return pl.pallas_call(
        kernel,
        in_specs=[pl.BlockSpec(memory_space=pltpu.VMEM)] * len(vmem)
        + [pl.BlockSpec(memory_space=pltpu.HBM)] * len(hbm),
        out_specs=[pl.BlockSpec(memory_space=pltpu.VMEM)] * len(outs),
        out_shape=[jax.ShapeDtypeStruct(shape, BF) for shape in outs],
        scratch_shapes=[pltpu.VMEM(shape, BF) for shape in scratch]
        + [pltpu.SemaphoreType.DMA((3 * D // STEP + 1,))],
        compiler_params=pltpu.CompilerParams(vmem_limit_bytes=LIMIT),
        cost_estimate=estimate,
        name=name,
    )(*vmem, *hbm)


def time_kernel(perm_ref, x_ref, w_ref, wo_ref, *refs, k):
    outs, (xp_ref, normed_ref, qkv_ref, ctx_ref, w_held, wo_held, sems) = refs[:4], refs[4:]
    wait = start_weights(w_ref, w_held, sems, 0)
    last = pltpu.make_async_copy(wo_ref.at[0], wo_held, sems.at[3 * D // STEP])
    last.start()
    perm = perm_ref[...]
    for t in range(2):
        x = x_ref[:, 2 * k + t].reshape(GROUP, D)
        load_tokens(perm, x, xp_ref, normed_ref, t * GROUP)
    project(normed_ref, w_held, qkv_ref, wait)
    low, high = masks()
    for line in range(4):
        rows = slice(line * LINE, line * LINE + LINE)
        for p in range(PAIRS):
            at = p * 128
            q, k_, v = (qkv_ref[rows, part + at : part + at + 128] for part in (0, D, 2 * D))
            ctx_ref[rows, at : at + 128] = attend(q, k_, v, low, high, None)
    last.wait()
    for at in range(0, D, STEP):
        columns = slice(at, at + STEP)
        y = jnp.dot(ctx_ref[...], wo_held[:, columns], preferred_element_type=F32)
        y = (xp_ref[:, columns].astype(F32) + y).astype(BF)
        for r in range(4):
            for s in range(4):
                row = (r * 4 + s) * 32
                outs[s][r, :, columns] = y[row : row + 32]


def time_block(perm, lines, w_triple, w_out, k):
    tokens = 512
    return call(
        functools.partial(time_kernel, k=k),
        [perm, lines],
        [w_triple, w_out],
        [(4, 32, D)] * 4,
        [(tokens, D), (tokens, D), (tokens, 3 * D), (tokens, D), (D, 3 * D), (D, D)],
        cost(tokens, 4, tokens),
        f"time_block_{k}",
    )


def load_rows(pieces, xp_ref, normed_ref):
    o = lax.broadcasted_iota(jnp.int32, (LINE, LINE), 0)
    i = lax.broadcasted_iota(jnp.int32, (LINE, LINE), 1)
    perm = ((o % 16) * 8 + o // 16 == i).astype(F32).astype(BF)
    for n in range(4):
        x = [piece[r, n * 8 : n * 8 + 8, :] for piece in pieces for r in range(4)]
        load_tokens(perm, jnp.concatenate(x, axis=0), xp_ref, normed_ref, n * LINE)


def early_kernel(*refs):
    pieces, w_ref, qkv_ref, xp_ref = refs[:4], refs[4], refs[5], refs[6]
    normed_ref, w_held, sems = refs[7:]
    wait = start_weights(w_ref, w_held, sems, 1)
    load_rows(pieces, xp_ref, normed_ref)
    project(normed_ref, w_held, qkv_ref, wait)


def early(pieces, w_triple):
    tokens = 512
    return call(
        early_kernel,
        pieces,
        [w_triple],
        [(tokens, 3 * D), (tokens, D)],
        [(tokens, D), (D, 3 * D)],
        cost(tokens, 3, 0),
        "early",
    )


def height_kernel(*refs):
    perm_ref, qkv_a, xp_a, pieces, w_ref, wo_ref, y_ref = *refs[:3], refs[3:7], *refs[7:10]
    xp_b, normed_ref, qkv_b, ctx_ref, w_held, wo_held, sems = refs[10:]
    wait = start_weights(w_ref, w_held, sems, 1)
    last = pltpu.make_async_copy(wo_ref.at[1], wo_held, sems.at[3 * D // STEP])
    last.start()
    load_rows(pieces, xp_b, normed_ref)
    project(normed_ref, w_held, qkv_b, wait)
    low, high = masks()
    a = lax.broadcasted_iota(jnp.int32, (2 * LINE, LINE), 0) % 64 // 16
    b = lax.broadcasted_iota(jnp.int32, (2 * LINE, LINE), 1) % 64 // 16
    same = a == b

    @pl.loop(0, 8 // UNROLL)
    def _(n):
        for j in range(UNROLL):
            i = n * UNROLL + j
            rows = pl.ds(pl.multiple_of(i * 64, 64), 64)
            for p in range(PAIRS):
                q, k, v = (
                    jnp.concatenate(
                        [ref[rows, part * D + p * 128 : part * D + p * 128 + 128] for ref in (qkv_a, qkv_b)]
                    )
                    for part in range(3)
                )
                o = attend(q, k, v, low, high, same)
                for half in range(2):
                    at = (i // 2) * 256 + half * 128 + (i % 2) * 64
                    at = pl.ds(pl.multiple_of(at, 64), 64)
                    ctx_ref[at, p * 128 : p * 128 + 128] = o[half * 64 : half * 64 + 64]

    last.wait()
    for at in range(0, D, STEP):
        columns = slice(at, at + STEP)
        y = jnp.dot(ctx_ref[...], wo_held[:, columns], preferred_element_type=F32)
        for n in range(4):
            x = [xp[n * 128 : n * 128 + 128, columns] for xp in (xp_a, xp_b)]
            z = jnp.concatenate(x).astype(F32) + y[n * GROUP : n * GROUP + GROUP]
            z = jnp.dot(perm_ref[...], z.astype(BF), preferred_element_type=F32).astype(BF)
            y_ref[n * 8 : n * 8 + 8, :, columns] = z.reshape(8, 32, STEP)


def height_block(perm, qkv_a, xp_a, pieces, w_triple, w_out):
    tokens = 512
    return call(
        height_kernel,
        [perm, qkv_a, xp_a, *pieces],
        [w_triple, w_out],
        [(32, 32, D)],
        [(tokens, D), (tokens, D), (tokens, 3 * D), (2 * tokens, D), (D, 3 * D), (D, D)],
        cost(2 * tokens, 4, 2 * tokens),
        "height_block",
    )[0]


UNROLL = 4


def on_device(video, w_triple, w_out):
    g = lax.axis_index("grp")
    o = jnp.arange(GROUP)
    want = (o % 32) * 8 + (o // 128) * 4 + (((o // 32) % 4) ^ g)
    perm0 = permutation(want, o)
    want = ((o // 4) % 2) * 128 + (o // 32) * 16 + (((o // 8) % 4) ^ g) * 4 + o % 4
    perm1 = permutation(want, o)

    lines = lax.all_to_all(to_columns(video), "mem", split_axis=0, concat_axis=0, tiled=True)
    pieces = []
    for k in range(2):
        outs = time_block(perm0, lines, w_triple, w_out, k)
        pieces.append(
            [outs[0]]
            + [lax.ppermute(outs[s], "grp", [(i, i ^ s) for i in range(4)]) for s in range(1, 4)]
        )
    qkv, xp = early(pieces[0], w_triple)
    done = height_block(perm1, qkv, xp, pieces[1], w_triple, w_out)
    done = lax.all_to_all(
        done.reshape(128, 8, D), ("mem", "grp"), split_axis=0, concat_axis=0, tiled=True
    )
    return to_tokens(done.reshape(32, 4, 8, D))


def solution(mesh):
    return jax.shard_map(
        on_device,
        mesh=mesh,
        in_specs=(P("mem", "grp", None, None), P(), P()),
        out_specs=P("mem", "grp", None, None),
        check_vma=False,
    )
```

time: 391 us -> 133 us (0.34); the launches traced: 384 us -> 133 us
  blocking collectives: 224 us -> 37 us
  local copies, waits for them, and re-layouts: 96 us -> 0 us
  matrix products: 46.4 us -> 0 us
  Pallas kernels: 0 us -> 44.5 us
  waiting for transfers between devices: 0 us -> 33.8 us
  other arithmetic: 17.4 us -> 0.22 us
  starting transfers between devices: 0 us -> 17 us
    all_to_all x4 -> x1, blocking collectives: 224 us -> 37 us  [on_device(): lax.all_to_all(done.reshape(128, 8, D), ('mem', 'grp'), split_axis=0, con...]
    reshape x7 -> x0, local copies, waits for them, and re-layouts: 52.1 us -> none  [the longest x2 31.9 us: attend_local(): pieces = triple.reshape(lead + (3, HEADS, HEAD))]
    dot_general x8 -> x0, matrix products: 46.4 us -> none  [the longest x2 19.3 us: make_triple(): jnp.dot(normed.reshape(-1, width), weight_in, preferred_element_type=jnp....]
    pallas_call x0 -> x6, Pallas kernels: none -> 44.5 us  [the longest x4 39.7 us: call(): pl.pallas_call(kernel, in_specs=[pl.BlockSpec(memory_space=pltpu.VMEM)] *...]
    all_to_all x0 -> x1, waiting for transfers between devices: none -> 28.9 us  [on_device(): lax.all_to_all(to_columns(video), 'mem', split_axis=0, concat_axis=0, til...]
    unnamed x13 -> x0, local copies, waits for them, and re-layouts: 19.6 us -> none
    slice x2 -> x0, local copies, waits for them, and re-layouts: 17.5 us -> none  [attend_local(): values = pieces[..., 2, :, :]]
    sub x2 -> x0, other arithmetic: 12.9 us -> none  [attend_local(): expo = jnp.exp(scores - top)]
  transfers between devices with their start and end apart: 0 -> 7, of which waited for: 0 -> 3; matrix products, arithmetic and copies ran while one was open for 0% -> 0% of each run, Pallas kernels for 0% -> 12%
where the time goes in v3:
time: 133 us
  Pallas kernels  44.5 us (33%)
  blocking collectives  37 us (28%)
  waiting for transfers between devices  33.8 us (25%)
  starting transfers between devices  17 us (13%)
    pallas_call x4, Pallas kernels, call(): pl.pallas_call(kernel, in_specs=[pl.BlockSpec(memory_space=pltpu.VMEM)] *...  39.7 us
    all_to_all x1, blocking collectives, on_device(): lax.all_to_all(done.reshape(128, 8, D), ('mem', 'grp'), split_axis=0, con...  37 us
    all_to_all x1, waiting for transfers between devices, on_device(): lax.all_to_all(to_columns(video), 'mem', split_axis=0, concat_axis=0, til...  28.9 us
    all_to_all x1, starting transfers between devices, on_device(): lax.all_to_all(to_columns(video), 'mem', split_axis=0, concat_axis=0, til...  11.4 us
    ppermute x6, starting transfers between devices, on_device(): lax.ppermute(outs[s], 'grp', [(i, i ^ s) for i in range(4)])  5.67 us
    ppermute x6, waiting for transfers between devices, on_device(): lax.ppermute(outs[s], 'grp', [(i, i ^ s) for i in range(4)])  4.88 us
    pallas_call x1, Pallas kernels, to_columns(): pl.pallas_call(to_columns_kernel, in_specs=[pl.BlockSpec(memory_space=plt...  3.12 us
  transfers between devices with their start and end apart: 7, of which 3 were waited for; matrix products, arithmetic and copies ran while one was open for 0% of the time, Pallas kernels for 12%

profile of v3, /device:TPU:1, one launch (start us, length us, event | category | flops | bytes accessed | tf_op | source)
XLA Modules:
  0.0 132.9 jit_solution(7558769902305533312)
XLA Ops:
  0.0 3.1 %to_columns.1 = bf16[32,4,8,1024]{3,2,1,0:T(8,128)(2,1)} custom-call(bf16[4,8,32,1024]{3,2,1,0:T(8,128)(2,1)} %x_ref.1), custom_call_target="tpu_custom_call" | custom-call | tf_op jit(solution)/shard_map/to_columns/pallas_call | solution.py:58
  3.1 11.4 %all-to-all-start = ((bf16[32,4,8,1024]{3,2,1,0:T(8,128)(2,1)}), bf16[32,4,8,1024]{3,2,1,0:T(8,128)(2,1)S(1)}, u32[]{:S(2)}, u32[]{:S(2)}) async-start(bf16[32,4,8,1024]{3,2,1,0:T(8,128)(2,1)} %to_columns.1), calls=%async_computation | async-start | bytes 4194304 | tf_op jit(solution)/shard_map/all_to_all | solution.py:311
  14.5 0.1 fusion.1.perm_ref
  14.6 0.1 fusion.refs_0_
  14.7 28.9 %all-to-all-done.x_ref = bf16[32,4,8,1024]{3,2,1,0:T(8,128)(2,1)S(1)} async-done(((bf16[32,4,8,1024]{3,2,1,0:T(8,128)(2,1)}), bf16[32,4,8,1024]{3,2,1,0:T(8,128)(2,1)S(1)}, u32[]{:S(2)}, u32[]{:S(2)}) %all-to-all-start) | async-done | bytes 2097184 | tf_op jit(solution)/shard_map/all_to_all | solution.py:311
  43.7 8.6 %time_block_0.1 = (bf16[4,32,1024]{2,1,0:T(8,128)(2,1)S(1)}, bf16[4,32,1024]{2,1,0:T(8,128)(2,1)S(1)}, bf16[4,32,1024]{2,1,0:T(8,128)(2,1)S(1)}, bf16[4,32,1024]{2,1,0:T(8,128)(2,1)S(1)}) custom-call(bf16[256,256]{1,0:T(8,128)(2,1)S(1)} %fusion.1.perm_ref, bf16[32,4,8,1024]{3,2,1,0:T(8,128)(2,1)S(1)} %all-to-all-done.x_ref, bf16[2,1024,3072]{2,1,0:T(8,128)(2,1)} %refs_7_.1, ...), custom_call_target="tpu_custom_call" | custom-call | flops 4563402752 | bytes 8388608 | tf_op jit(solution)/shard_map/time_block_0/pallas_call | solution.py:160
  52.3 1.7 %collective-permute-start = (bf16[4,32,1024]{2,1,0:T(8,128)(2,1)S(1)}, bf16[4,32,1024]{2,1,0:T(8,128)(2,1)S(1)}, u32[]{:S(2)}, u32[]{:S(2)}) collective-permute-start(bf16[4,32,1024]{2,1,0:T(8,128)(2,1)S(1)} %get-tuple-element.16), channel_id=1, source_target_pairs={{0,32},{32,0},{64,96},{96,64},{1,33},{33,1},{65,97},{97,65},{2,34}... | collective-permute-start | bytes 786440 | tf_op jit(solution)/shard_map/ppermute | solution.py:317
  54.0 1.3 collective-permute-start.1
  55.3 0.4 collective-permute-start.2
  55.7 8.6 %time_block_1.1 = (bf16[4,32,1024]{2,1,0:T(8,128)(2,1)S(1)}, bf16[4,32,1024]{2,1,0:T(8,128)(2,1)S(1)}, bf16[4,32,1024]{2,1,0:T(8,128)(2,1)S(1)}, bf16[4,32,1024]{2,1,0:T(8,128)(2,1)S(1)}) custom-call(bf16[256,256]{1,0:T(8,128)(2,1)S(1)} %fusion.1.perm_ref, bf16[32,4,8,1024]{3,2,1,0:T(8,128)(2,1)S(1)} %all-to-all-done.x_ref, bf16[2,1024,3072]{2,1,0:T(8,128)(2,1)} %refs_7_.1, ...), custom_call_target="tpu_custom_call" | custom-call | flops 4563402752 | bytes 8388608 | tf_op jit(solution)/shard_map/time_block_1/pallas_call | solution.py:160
  64.4 0.2 collective-permute-start.3
  64.6 1.3 collective-permute-start.4
  65.9 0.0 collective-permute-done.refs_1_
  65.9 0.7 collective-permute-start.5
  66.6 0.0 collective-permute-done.1.refs_2_
  66.6 1.6 %collective-permute-done.2.refs_3_ = bf16[4,32,1024]{2,1,0:T(8,128)(2,1)S(1)} collective-permute-done((bf16[4,32,1024]{2,1,0:T(8,128)(2,1)S(1)}, bf16[4,32,1024]{2,1,0:T(8,128)(2,1)S(1)}, u32[]{:S(2)}, u32[]{:S(2)}) %collective-permute-start.2) | collective-permute-done | bytes 262176 | tf_op jit(solution)/shard_map/ppermute | solution.py:317
  68.2 7.4 %early.1 = (bf16[512,3072]{1,0:T(8,128)(2,1)}, bf16[512,1024]{1,0:T(8,128)(2,1)S(1)}) custom-call(bf16[4,32,1024]{2,1,0:T(8,128)(2,1)S(1)} %get-tuple-element.15.refs_0_, bf16[4,32,1024]{2,1,0:T(8,128)(2,1)S(1)} %collective-permute-done.refs_1_, bf16[4,32,1024]{2,1,0:T(8,128)(2,1)S(1)} %collective-permute-done.1.refs_2_, ...), custom_call_target="tpu_custom_call" | custom-call | flops 3221225472 | bytes 6291456 | tf_op jit(solution)/shard_map/early/pallas_call | solution.py:160
  75.6 0.0 collective-permute-done.3.refs_4_
  75.6 0.0 collective-permute-done.4.refs_5_
  75.6 3.3 %collective-permute-done.5.refs_6_ = bf16[4,32,1024]{2,1,0:T(8,128)(2,1)S(1)} collective-permute-done((bf16[4,32,1024]{2,1,0:T(8,128)(2,1)S(1)}, bf16[4,32,1024]{2,1,0:T(8,128)(2,1)S(1)}, u32[]{:S(2)}, u32[]{:S(2)}) %collective-permute-start.5) | collective-permute-done | bytes 262176 | tf_op jit(solution)/shard_map/ppermute | solution.py:317
  78.9 15.1 %height_block.1 = bf16[32,32,1024]{2,1,0:T(8,128)(2,1)} custom-call(bf16[256,256]{1,0:T(8,128)(2,1)S(1)} %fusion.refs_0_, bf16[512,3072]{1,0:T(8,128)(2,1)} %get-tuple-element.19.refs_1_, bf16[512,1024]{1,0:T(8,128)(2,1)S(1)} %get-tuple-element.20.refs_2_, bf16[4,32,1024]{2,1,0:T(8,128)(2,1)S(1)} %get-tuple-element.21.refs_3_, ...), custom_call_target="tpu_custom_call" | custom-call | flops 9126805504 | bytes 8388608 | tf_op jit(solution)/shard_map/height_block/pallas_call | solution.py:160
  94.0 37.0 %all_to_all.10 = bf16[128,8,1024]{2,1,0:T(8,128)(2,1)S(1)} all-to-all(bf16[128,8,1024]{2,1,0:T(8,128)(2,1)} %bitcast.3), channel_id=1, replica_groups=mesh['grp'=4,'mem'=32] {'mem','grp'}, dimensions={0} | all-to-all | bytes 4194304 | tf_op jit(solution)/shard_map/all_to_all | solution.py:321
  131.0 1.6 %to_tokens.1 = bf16[4,8,32,1024]{3,2,1,0:T(8,128)(2,1)} custom-call(bf16[32,4,8,1024]{3,2,1,0:T(8,128)(2,1)S(1)} %bitcast.2), custom_call_target="tpu_custom_call" | custom-call | tf_op jit(solution)/shard_map/to_tokens/pallas_call | solution.py:86
  (2 shorter events, 0.0 us)
Async XLA Ops:
  3.1 40.6 %all-to-all-start = ((bf16[32,4,8,1024]{3,2,1,0:T(8,128)(2,1)}), bf16[32,4,8,1024]{3,2,1,0:T(8,128)(2,1)S(1)}, u32[]{:S(2)}, u32[]{:S(2)}) async-start(bf16[32,4,8,1024]{3,2,1,0:T(8,128)(2,1)} %to_columns.1), calls=%async_computation | async-start | bytes 4194304 | tf_op jit(solution)/shard_map/all_to_all | solution.py:311
  52.3 13.6 %collective-permute-start = (bf16[4,32,1024]{2,1,0:T(8,128)(2,1)S(1)}, bf16[4,32,1024]{2,1,0:T(8,128)(2,1)S(1)}, u32[]{:S(2)}, u32[]{:S(2)}) collective-permute-start(bf16[4,32,1024]{2,1,0:T(8,128)(2,1)S(1)} %get-tuple-element.16), channel_id=1, source_target_pairs={{0,32},{32,0},{64,96},{96,64},{1,33},{33,1},{65,97},{97,65},{2,34}... | collective-permute-start | bytes 786440 | tf_op jit(solution)/shard_map/ppermute | solution.py:317
  54.0 12.6 %collective-permute-start.1 = (bf16[4,32,1024]{2,1,0:T(8,128)(2,1)S(1)}, bf16[4,32,1024]{2,1,0:T(8,128)(2,1)S(1)}, u32[]{:S(2)}, u32[]{:S(2)}) collective-permute-start(bf16[4,32,1024]{2,1,0:T(8,128)(2,1)S(1)} %get-tuple-element.17), channel_id=1, source_target_pairs={{0,64},{32,96},{64,0},{96,32},{1,65},{33,97},{65,1},{97,33},{2,66}... | collective-permute-start | bytes 786440 | tf_op jit(solution)/shard_map/ppermute | solution.py:317
  55.3 12.9 %collective-permute-start.2 = (bf16[4,32,1024]{2,1,0:T(8,128)(2,1)S(1)}, bf16[4,32,1024]{2,1,0:T(8,128)(2,1)S(1)}, u32[]{:S(2)}, u32[]{:S(2)}) collective-permute-start(bf16[4,32,1024]{2,1,0:T(8,128)(2,1)S(1)} %get-tuple-element.18), channel_id=1, source_target_pairs={{0,96},{32,64},{64,32},{96,0},{1,97},{33,65},{65,33},{97,1},{2,98}... | collective-permute-start | bytes 786440 | tf_op jit(solution)/shard_map/ppermute | solution.py:317
  64.4 11.2 %collective-permute-start.3 = (bf16[4,32,1024]{2,1,0:T(8,128)(2,1)S(1)}, bf16[4,32,1024]{2,1,0:T(8,128)(2,1)S(1)}, u32[]{:S(2)}, u32[]{:S(2)}) collective-permute-start(bf16[4,32,1024]{2,1,0:T(8,128)(2,1)S(1)} %get-tuple-element.22), channel_id=1, source_target_pairs={{0,32},{32,0},{64,96},{96,64},{1,33},{33,1},{65,97},{97,65},{2,34}... | collective-permute-start | bytes 786440 | tf_op jit(solution)/shard_map/ppermute | solution.py:317
  64.6 11.0 %collective-permute-start.4 = (bf16[4,32,1024]{2,1,0:T(8,128)(2,1)S(1)}, bf16[4,32,1024]{2,1,0:T(8,128)(2,1)S(1)}, u32[]{:S(2)}, u32[]{:S(2)}) collective-permute-start(bf16[4,32,1024]{2,1,0:T(8,128)(2,1)S(1)} %get-tuple-element.23), channel_id=1, source_target_pairs={{0,64},{32,96},{64,0},{96,32},{1,65},{33,97},{65,1},{97,33},{2,66}... | collective-permute-start | bytes 786440 | tf_op jit(solution)/shard_map/ppermute | solution.py:317
  65.9 13.1 %collective-permute-start.5 = (bf16[4,32,1024]{2,1,0:T(8,128)(2,1)S(1)}, bf16[4,32,1024]{2,1,0:T(8,128)(2,1)S(1)}, u32[]{:S(2)}, u32[]{:S(2)}) collective-permute-start(bf16[4,32,1024]{2,1,0:T(8,128)(2,1)S(1)} %get-tuple-element.24), channel_id=1, source_target_pairs={{0,96},{32,64},{64,32},{96,0},{1,97},{33,65},{65,33},{97,1},{2,98}... | collective-permute-start | bytes 786440 | tf_op jit(solution)/shard_map/ppermute | solution.py:317

commit v4 on v3

--- a/solution.py
+++ b/solution.py
@@ -20,6 +20,8 @@
 LINE = 128
 GROUP = 256
 LIMIT = 50 * 2**20
+EARLY_LIMIT = 44 * 2**20
+HEIGHT_LIMIT = 36 * 2**20
 STEP = 512
 
 
@@ -156,7 +158,7 @@
     )
 
 
-def call(kernel, vmem, hbm, outs, scratch, estimate, name):
+def call(kernel, vmem, hbm, outs, scratch, estimate, name, limit=LIMIT):
     return pl.pallas_call(
         kernel,
         in_specs=[pl.BlockSpec(memory_space=pltpu.VMEM)] * len(vmem)
@@ -165,7 +167,7 @@
         out_shape=[jax.ShapeDtypeStruct(shape, BF) for shape in outs],
         scratch_shapes=[pltpu.VMEM(shape, BF) for shape in scratch]
         + [pltpu.SemaphoreType.DMA((3 * D // STEP + 1,))],
-        compiler_params=pltpu.CompilerParams(vmem_limit_bytes=LIMIT),
+        compiler_params=pltpu.CompilerParams(vmem_limit_bytes=limit),
         cost_estimate=estimate,
         name=name,
     )(*vmem, *hbm)
@@ -212,88 +214,97 @@
     )
 
 
-def load_rows(pieces, xp_ref, normed_ref):
-    o = lax.broadcasted_iota(jnp.int32, (LINE, LINE), 0)
-    i = lax.broadcasted_iota(jnp.int32, (LINE, LINE), 1)
-    perm = ((o % 16) * 8 + o // 16 == i).astype(F32).astype(BF)
+def load_rows(pieces, xp_ref, normed_ref, start):
+    frame = 4 * len(pieces)
+    span = 8 * frame
+    o = lax.broadcasted_iota(jnp.int32, (span, span), 0)
+    i = lax.broadcasted_iota(jnp.int32, (span, span), 1)
+    perm = ((o % frame) * 8 + o // frame == i).astype(F32).astype(BF)
     for n in range(4):
         x = [piece[r, n * 8 : n * 8 + 8, :] for piece in pieces for r in range(4)]
-        load_tokens(perm, jnp.concatenate(x, axis=0), xp_ref, normed_ref, n * LINE)
+        load_tokens(perm, jnp.concatenate(x, axis=0), xp_ref, normed_ref, start + n * span)
+
+
+EARLY = 768
+LATE = 256
 
 
 def early_kernel(*refs):
-    pieces, w_ref, qkv_ref, xp_ref = refs[:4], refs[4], refs[5], refs[6]
-    normed_ref, w_held, sems = refs[7:]
+    pieces, w_ref, qkv_ref, xp_ref = refs[:6], refs[6], refs[7], refs[8]
+    normed_ref, w_held, sems = refs[9:]
     wait = start_weights(w_ref, w_held, sems, 1)
-    load_rows(pieces, xp_ref, normed_ref)
+    load_rows(pieces[:4], xp_ref, normed_ref, 0)
+    load_rows(pieces[4:], xp_ref, normed_ref, 512)
     project(normed_ref, w_held, qkv_ref, wait)
 
 
 def early(pieces, w_triple):
-    tokens = 512
     return call(
         early_kernel,
         pieces,
         [w_triple],
-        [(tokens, 3 * D), (tokens, D)],
-        [(tokens, D), (D, 3 * D)],
-        cost(tokens, 3, 0),
+        [(EARLY, 3 * D), (EARLY, D)],
+        [(EARLY, D), (D, 3 * D)],
+        cost(EARLY, 3, 0),
         "early",
+        EARLY_LIMIT,
     )
 
 
 def height_kernel(*refs):
-    perm_ref, qkv_a, xp_a, pieces, w_ref, wo_ref, y_ref = *refs[:3], refs[3:7], *refs[7:10]
-    xp_b, normed_ref, qkv_b, ctx_ref, w_held, wo_held, sems = refs[10:]
+    perm_ref, qkv_a, xp_a, pieces, w_ref, wo_ref, y_ref = *refs[:3], refs[3:5], *refs[5:8]
+    xp_b, normed_ref, qkv_b, ctx_ref, w_held, wo_held, sems = refs[8:]
     wait = start_weights(w_ref, w_held, sems, 1)
     last = pltpu.make_async_copy(wo_ref.at[1], wo_held, sems.at[3 * D // STEP])
     last.start()
-    load_rows(pieces, xp_b, normed_ref)
+    load_rows(pieces, xp_b, normed_ref, 0)
     project(normed_ref, w_held, qkv_b, wait)
+
+    def run(early, late, i, columns):
+        at = lambda base, size: pl.ds(pl.multiple_of(base + i * size, size), size)
+        parts = [early[at(0, 64), columns], early[at(512, 32), columns], late[at(0, 32), columns]]
+        return jnp.concatenate(parts, axis=0)
+
+    def frame(shape, axis):
+        t = lax.broadcasted_iota(jnp.int32, shape, axis) % LINE
+        return jnp.where(t < 64, t // 16, t % 32 // 8)
+
     low, high = masks()
-    a = lax.broadcasted_iota(jnp.int32, (2 * LINE, LINE), 0) % 64 // 16
-    b = lax.broadcasted_iota(jnp.int32, (2 * LINE, LINE), 1) % 64 // 16
-    same = a == b
+    same = frame((2 * LINE, LINE), 0) == frame((2 * LINE, LINE), 1)
 
     @pl.loop(0, 8 // UNROLL)
     def _(n):
         for j in range(UNROLL):
             i = n * UNROLL + j
-            rows = pl.ds(pl.multiple_of(i * 64, 64), 64)
-            for p in range(PAIRS):
+            rows = pl.ds(pl.multiple_of(i * LINE, LINE), LINE)
+            for at in range(0, D, 128):
                 q, k, v = (
-                    jnp.concatenate(
-                        [ref[rows, part * D + p * 128 : part * D + p * 128 + 128] for ref in (qkv_a, qkv_b)]
-                    )
-                    for part in range(3)
+                    run(qkv_a, qkv_b, i, slice(part + at, part + at + 128))
+                    for part in (0, D, 2 * D)
                 )
-                o = attend(q, k, v, low, high, same)
-                for half in range(2):
-                    at = (i // 2) * 256 + half * 128 + (i % 2) * 64
-                    at = pl.ds(pl.multiple_of(at, 64), 64)
-                    ctx_ref[at, p * 128 : p * 128 + 128] = o[half * 64 : half * 64 + 64]
+                ctx_ref[rows, at : at + 128] = attend(q, k, v, low, high, same)
 
     last.wait()
     for at in range(0, D, STEP):
         columns = slice(at, at + STEP)
         y = jnp.dot(ctx_ref[...], wo_held[:, columns], preferred_element_type=F32)
         for n in range(4):
-            x = [xp[n * 128 : n * 128 + 128, columns] for xp in (xp_a, xp_b)]
-            z = jnp.concatenate(x).astype(F32) + y[n * GROUP : n * GROUP + GROUP]
+            x = jnp.concatenate([run(xp_a, xp_b, i, columns) for i in (2 * n, 2 * n + 1)], axis=0)
+            z = x.astype(F32) + y[n * GROUP : n * GROUP + GROUP]
             z = jnp.dot(perm_ref[...], z.astype(BF), preferred_element_type=F32).astype(BF)
             y_ref[n * 8 : n * 8 + 8, :, columns] = z.reshape(8, 32, STEP)
 
 
 def height_block(perm, qkv_a, xp_a, pieces, w_triple, w_out):
-    tokens = 512
     return call(
         height_kernel,
         [perm, qkv_a, xp_a, *pieces],
         [w_triple, w_out],
         [(32, 32, D)],
-        [(tokens, D), (tokens, D), (tokens, 3 * D), (2 * tokens, D), (D, 3 * D), (D, D)],
-        cost(2 * tokens, 4, 2 * tokens),
+        [(LATE, D), (LATE, D), (LATE, 3 * D), (1024, D), (D, 3 * D), (D, D)],
+        cost(1024, 3, 1024),
         "height_block",
+        HEIGHT_LIMIT,
     )[0]
 
 
@@ -305,8 +316,10 @@
     o = jnp.arange(GROUP)
     want = (o % 32) * 8 + (o // 128) * 4 + (((o // 32) % 4) ^ g)
     perm0 = permutation(want, o)
-    want = ((o // 4) % 2) * 128 + (o // 32) * 16 + (((o // 8) % 4) ^ g) * 4 + o % 4
-    perm1 = permutation(want, o)
+    m, s, chunk, r = o // 32, ((o // 8) % 4) ^ g, (o // 4) % 2, o % 4
+    first = (m % 4) * 16 + s * 4 + r
+    second = 64 + (s // 2) * 32 + (m % 4) * 8 + (s % 2) * 4 + r
+    perm1 = permutation((m // 4) * LINE + jnp.where(chunk == 0, first, second), o)
 
     lines = lax.all_to_all(to_columns(video), "mem", split_axis=0, concat_axis=0, tiled=True)
     pieces = []
@@ -316,8 +329,10 @@
             [outs[0]]
             + [lax.ppermute(outs[s], "grp", [(i, i ^ s) for i in range(4)]) for s in range(1, 4)]
         )
-    qkv, xp = early(pieces[0], w_triple)
-    done = height_block(perm1, qkv, xp, pieces[1], w_triple, w_out)
+        if k == 0:
+            lines, pieces[0][0] = lax.optimization_barrier((lines, pieces[0][0]))
+    qkv, xp = early(pieces[0] + pieces[1][:2], w_triple)
+    done = height_block(perm1, qkv, xp, pieces[1][2:], w_triple, w_out)
     done = lax.all_to_all(
         done.reshape(128, 8, D), ("mem", "grp"), split_axis=0, concat_axis=0, tiled=True
     )

time: 133 us -> 128 us (0.962)
  Pallas kernels: 44.5 us -> 40.2 us
    pallas_call x4, Pallas kernels: 39.7 us -> 35.5 us  [call(): pl.pallas_call(kernel, in_specs=[pl.BlockSpec(memory_space=pltpu.VMEM)] *...]
  transfers between devices with their start and end apart: 7 -> 7, of which waited for: 3 -> 3; matrix products, arithmetic and copies ran while one was open for 0% -> 0% of each run, Pallas kernels for 12% -> 13%
where the time goes in v4:
time: 128 us
  Pallas kernels  40.2 us (31%)
  blocking collectives  36.9 us (29%)
  waiting for transfers between devices  32.9 us (26%)
  starting transfers between devices  17.1 us (13%)
    all_to_all x1, blocking collectives, on_device(): lax.all_to_all(done.reshape(128, 8, D), ('mem', 'grp'), split_axis=0, con...  36.9 us
    pallas_call x4, Pallas kernels, call(): pl.pallas_call(kernel, in_specs=[pl.BlockSpec(memory_space=pltpu.VMEM)] *...  35.5 us
    all_to_all x1, waiting for transfers between devices, on_device(): lax.all_to_all(to_columns(video), 'mem', split_axis=0, concat_axis=0, til...  29.1 us
    all_to_all x1, starting transfers between devices, on_device(): lax.all_to_all(to_columns(video), 'mem', split_axis=0, concat_axis=0, til...  11.4 us
    ppermute x6, starting transfers between devices, on_device(): lax.ppermute(outs[s], 'grp', [(i, i ^ s) for i in range(4)])  5.75 us
    ppermute x6, waiting for transfers between devices, on_device(): lax.ppermute(outs[s], 'grp', [(i, i ^ s) for i in range(4)])  3.83 us
    pallas_call x1, Pallas kernels, to_columns(): pl.pallas_call(to_columns_kernel, in_specs=[pl.BlockSpec(memory_space=plt...  3.12 us
  transfers between devices with their start and end apart: 7, of which 3 were waited for; matrix products, arithmetic and copies ran while one was open for 0% of the time, Pallas kernels for 13%

profile of v4, /device:TPU:1, one launch (start us, length us, event | category | flops | bytes accessed | tf_op | source)
XLA Modules:
  0.0 127.7 jit_solution(13675989062502096059)
XLA Ops:
  0.0 3.1 %to_columns.1 = bf16[32,4,8,1024]{3,2,1,0:T(8,128)(2,1)} custom-call(bf16[4,8,32,1024]{3,2,1,0:T(8,128)(2,1)} %x_ref.1), custom_call_target="tpu_custom_call" | custom-call | tf_op jit(solution)/shard_map/to_columns/pallas_call | solution.py:60
  3.1 11.4 %all-to-all-start = ((bf16[32,4,8,1024]{3,2,1,0:T(8,128)(2,1)}), bf16[32,4,8,1024]{3,2,1,0:T(8,128)(2,1)S(1)}, u32[]{:S(2)}, u32[]{:S(2)}) async-start(bf16[32,4,8,1024]{3,2,1,0:T(8,128)(2,1)} %to_columns.1), calls=%async_computation | async-start | bytes 4194304 | tf_op jit(solution)/shard_map/all_to_all | solution.py:324
  14.5 0.1 fusion.1.perm_ref
  14.6 29.1 %all-to-all-done.x_ref = bf16[32,4,8,1024]{3,2,1,0:T(8,128)(2,1)S(1)} async-done(((bf16[32,4,8,1024]{3,2,1,0:T(8,128)(2,1)}), bf16[32,4,8,1024]{3,2,1,0:T(8,128)(2,1)S(1)}, u32[]{:S(2)}, u32[]{:S(2)}) %all-to-all-start) | async-done | bytes 2097184 | tf_op jit(solution)/shard_map/all_to_all | solution.py:324
  43.7 8.6 %time_block_0.1 = (bf16[4,32,1024]{2,1,0:T(8,128)(2,1)S(1)}, bf16[4,32,1024]{2,1,0:T(8,128)(2,1)S(1)}, bf16[4,32,1024]{2,1,0:T(8,128)(2,1)S(1)}, bf16[4,32,1024]{2,1,0:T(8,128)(2,1)S(1)}) custom-call(bf16[256,256]{1,0:T(8,128)(2,1)S(1)} %fusion.1.perm_ref, bf16[32,4,8,1024]{3,2,1,0:T(8,128)(2,1)S(1)} %all-to-all-done.x_ref, bf16[2,1024,3072]{2,1,0:T(8,128)(2,1)} %refs_5_.1, ...), custom_call_target="tpu_custom_call" | custom-call | flops 4563402752 | bytes 8388608 | tf_op jit(solution)/shard_map/time_block_0/pallas_call | solution.py:162
  52.3 1.7 %collective-permute-start = (bf16[4,32,1024]{2,1,0:T(8,128)(2,1)S(1)}, bf16[4,32,1024]{2,1,0:T(8,128)(2,1)S(1)}, u32[]{:S(2)}, u32[]{:S(2)}) collective-permute-start(bf16[4,32,1024]{2,1,0:T(8,128)(2,1)S(1)} %get-tuple-element.19), channel_id=1, source_target_pairs={{0,32},{32,0},{64,96},{96,64},{1,33},{33,1},{65,97},{97,65},{2,34}... | collective-permute-start | bytes 786440 | tf_op jit(solution)/shard_map/ppermute | solution.py:330
  54.0 1.3 %collective-permute-start.1 = (bf16[4,32,1024]{2,1,0:T(8,128)(2,1)S(1)}, bf16[4,32,1024]{2,1,0:T(8,128)(2,1)S(1)}, u32[]{:S(2)}, u32[]{:S(2)}) collective-permute-start(bf16[4,32,1024]{2,1,0:T(8,128)(2,1)S(1)} %get-tuple-element.20), channel_id=1, source_target_pairs={{0,64},{32,96},{64,0},{96,32},{1,65},{33,97},{65,1},{97,33},{2,66}... | collective-permute-start | bytes 786440 | tf_op jit(solution)/shard_map/ppermute | solution.py:330
  55.3 0.4 collective-permute-start.2
  55.7 8.6 %time_block_1.1 = (bf16[4,32,1024]{2,1,0:T(8,128)(2,1)S(1)}, bf16[4,32,1024]{2,1,0:T(8,128)(2,1)S(1)}, bf16[4,32,1024]{2,1,0:T(8,128)(2,1)S(1)}, bf16[4,32,1024]{2,1,0:T(8,128)(2,1)S(1)}) custom-call(bf16[256,256]{1,0:T(8,128)(2,1)S(1)} %fusion.1.perm_ref, bf16[32,4,8,1024]{3,2,1,0:T(8,128)(2,1)S(1)} %all-to-all-done.x_ref, bf16[2,1024,3072]{2,1,0:T(8,128)(2,1)} %refs_5_.1, ...), custom_call_target="tpu_custom_call" | custom-call | flops 4563402752 | bytes 8388608 | tf_op jit(solution)/shard_map/time_block_1/pallas_call | solution.py:162
  64.4 0.2 collective-permute-start.3
  64.6 0.1 fusion.refs_0_
  64.7 1.3 %collective-permute-start.4 = (bf16[4,32,1024]{2,1,0:T(8,128)(2,1)S(1)}, bf16[4,32,1024]{2,1,0:T(8,128)(2,1)S(1)}, u32[]{:S(2)}, u32[]{:S(2)}) collective-permute-start(bf16[4,32,1024]{2,1,0:T(8,128)(2,1)S(1)} %get-tuple-element.27), channel_id=1, source_target_pairs={{0,64},{32,96},{64,0},{96,32},{1,65},{33,97},{65,1},{97,33},{2,66}... | collective-permute-start | bytes 786440 | tf_op jit(solution)/shard_map/ppermute | solution.py:330
  66.1 0.0 collective-permute-done.refs_1_
  66.1 0.7 collective-permute-start.5
  66.8 0.0 collective-permute-done.1.refs_2_
  66.8 1.3 %collective-permute-done.2.refs_3_ = bf16[4,32,1024]{2,1,0:T(8,128)(2,1)S(1)} collective-permute-done((bf16[4,32,1024]{2,1,0:T(8,128)(2,1)S(1)}, bf16[4,32,1024]{2,1,0:T(8,128)(2,1)S(1)}, u32[]{:S(2)}, u32[]{:S(2)}) %collective-permute-start.2) | collective-permute-done | bytes 262176 | tf_op jit(solution)/shard_map/ppermute | solution.py:330
  68.1 0.0 collective-permute-done.3.refs_5_
  68.1 0.0 copy-start
  68.1 8.3 %early.1 = (bf16[768,3072]{1,0:T(8,128)(2,1)S(1)}, bf16[768,1024]{1,0:T(8,128)(2,1)S(1)}) custom-call(bf16[4,32,1024]{2,1,0:T(8,128)(2,1)S(1)} %get-tuple-element.18.refs_0_, bf16[4,32,1024]{2,1,0:T(8,128)(2,1)S(1)} %collective-permute-done.refs_1_, bf16[4,32,1024]{2,1,0:T(8,128)(2,1)S(1)} %collective-permute-done.1.refs_2_, ...), custom_call_target="tpu_custom_call" | custom-call | flops 4831838208 | bytes 6291456 | tf_op jit(solution)/shard_map/early/pallas_call | solution.py:162
  76.4 0.0 collective-permute-done.4.refs_3_
  76.4 2.5 %collective-permute-done.5.refs_4_ = bf16[4,32,1024]{2,1,0:T(8,128)(2,1)S(1)} collective-permute-done((bf16[4,32,1024]{2,1,0:T(8,128)(2,1)S(1)}, bf16[4,32,1024]{2,1,0:T(8,128)(2,1)S(1)}, u32[]{:S(2)}, u32[]{:S(2)}) %collective-permute-start.5) | collective-permute-done | bytes 262176 | tf_op jit(solution)/shard_map/ppermute | solution.py:330
  78.9 0.0 copy-done
  78.9 10.0 %height_block.1 = bf16[32,32,1024]{2,1,0:T(8,128)(2,1)S(1)} custom-call(bf16[256,256]{1,0:T(8,128)(2,1)S(1)} %fusion.refs_0_, bf16[768,3072]{1,0:T(8,128)(2,1)S(1)} %get-tuple-element.25.refs_1_, bf16[768,1024]{1,0:T(8,128)(2,1)S(1)} %get-tuple-element.26.refs_2_, bf16[4,32,1024]{2,1,0:T(8,128)(2,1)S(1)} %collective-permute-done.4.refs_3_, ...), custom_call_target="tpu_custom_call" | custom-call | flops 6979321856 | bytes 6291456 | tf_op jit(solution)/shard_map/height_block/pallas_call | solution.py:162
  88.9 36.9 %all_to_all.10 = bf16[128,8,1024]{2,1,0:T(8,128)(2,1)S(1)} all-to-all(bf16[128,8,1024]{2,1,0:T(8,128)(2,1)S(1)} %bitcast.3), channel_id=1, replica_groups=mesh['grp'=4,'mem'=32] {'mem','grp'}, dimensions={0} | all-to-all | bytes 4194304 | tf_op jit(solution)/shard_map/all_to_all | solution.py:336
  125.8 1.6 %to_tokens.1 = bf16[4,8,32,1024]{3,2,1,0:T(8,128)(2,1)} custom-call(bf16[32,4,8,1024]{3,2,1,0:T(8,128)(2,1)S(1)} %bitcast.2), custom_call_target="tpu_custom_call" | custom-call | tf_op jit(solution)/shard_map/to_tokens/pallas_call | solution.py:88
  (2 shorter events, 0.0 us)
Async XLA Ops:
  3.1 40.6 %all-to-all-start = ((bf16[32,4,8,1024]{3,2,1,0:T(8,128)(2,1)}), bf16[32,4,8,1024]{3,2,1,0:T(8,128)(2,1)S(1)}, u32[]{:S(2)}, u32[]{:S(2)}) async-start(bf16[32,4,8,1024]{3,2,1,0:T(8,128)(2,1)} %to_columns.1), calls=%async_computation | async-start | bytes 4194304 | tf_op jit(solution)/shard_map/all_to_all | solution.py:324
  52.3 13.8 %collective-permute-start = (bf16[4,32,1024]{2,1,0:T(8,128)(2,1)S(1)}, bf16[4,32,1024]{2,1,0:T(8,128)(2,1)S(1)}, u32[]{:S(2)}, u32[]{:S(2)}) collective-permute-start(bf16[4,32,1024]{2,1,0:T(8,128)(2,1)S(1)} %get-tuple-element.19), channel_id=1, source_target_pairs={{0,32},{32,0},{64,96},{96,64},{1,33},{33,1},{65,97},{97,65},{2,34}... | collective-permute-start | bytes 786440 | tf_op jit(solution)/shard_map/ppermute | solution.py:330
  54.0 12.8 %collective-permute-start.1 = (bf16[4,32,1024]{2,1,0:T(8,128)(2,1)S(1)}, bf16[4,32,1024]{2,1,0:T(8,128)(2,1)S(1)}, u32[]{:S(2)}, u32[]{:S(2)}) collective-permute-start(bf16[4,32,1024]{2,1,0:T(8,128)(2,1)S(1)} %get-tuple-element.20), channel_id=1, source_target_pairs={{0,64},{32,96},{64,0},{96,32},{1,65},{33,97},{65,1},{97,33},{2,66}... | collective-permute-start | bytes 786440 | tf_op jit(solution)/shard_map/ppermute | solution.py:330
  55.3 12.8 %collective-permute-start.2 = (bf16[4,32,1024]{2,1,0:T(8,128)(2,1)S(1)}, bf16[4,32,1024]{2,1,0:T(8,128)(2,1)S(1)}, u32[]{:S(2)}, u32[]{:S(2)}) collective-permute-start(bf16[4,32,1024]{2,1,0:T(8,128)(2,1)S(1)} %get-tuple-element.21), channel_id=1, source_target_pairs={{0,96},{32,64},{64,32},{96,0},{1,97},{33,65},{65,33},{97,1},{2,98}... | collective-permute-start | bytes 786440 | tf_op jit(solution)/shard_map/ppermute | solution.py:330
  64.4 3.7 %collective-permute-start.3 = (bf16[4,32,1024]{2,1,0:T(8,128)(2,1)S(1)}, bf16[4,32,1024]{2,1,0:T(8,128)(2,1)S(1)}, u32[]{:S(2)}, u32[]{:S(2)}) collective-permute-start(bf16[4,32,1024]{2,1,0:T(8,128)(2,1)S(1)} %get-tuple-element.24), channel_id=1, source_target_pairs={{0,32},{32,0},{64,96},{96,64},{1,33},{33,1},{65,97},{97,65},{2,34}... | collective-permute-start | bytes 786440 | tf_op jit(solution)/shard_map/ppermute | solution.py:330
  64.7 11.7 %collective-permute-start.4 = (bf16[4,32,1024]{2,1,0:T(8,128)(2,1)S(1)}, bf16[4,32,1024]{2,1,0:T(8,128)(2,1)S(1)}, u32[]{:S(2)}, u32[]{:S(2)}) collective-permute-start(bf16[4,32,1024]{2,1,0:T(8,128)(2,1)S(1)} %get-tuple-element.27), channel_id=1, source_target_pairs={{0,64},{32,96},{64,0},{96,32},{1,65},{33,97},{65,1},{97,33},{2,66}... | collective-permute-start | bytes 786440 | tf_op jit(solution)/shard_map/ppermute | solution.py:330
  66.1 12.8 %collective-permute-start.5 = (bf16[4,32,1024]{2,1,0:T(8,128)(2,1)S(1)}, bf16[4,32,1024]{2,1,0:T(8,128)(2,1)S(1)}, u32[]{:S(2)}, u32[]{:S(2)}) collective-permute-start(bf16[4,32,1024]{2,1,0:T(8,128)(2,1)S(1)} %get-tuple-element.28), channel_id=1, source_target_pairs={{0,96},{32,64},{64,32},{96,0},{1,97},{33,65},{65,33},{97,1},{2,98}... | collective-permute-start | bytes 786440 | tf_op jit(solution)/shard_map/ppermute | solution.py:330
  68.1 10.8 %copy-start = (bf16[2,1024,1024]{2,1,0:T(8,128)(2,1)S(1)}, bf16[2,1024,1024]{2,1,0:T(8,128)(2,1)}, u32[]{:S(2)}) copy-start(bf16[2,1024,1024]{2,1,0:T(8,128)(2,1)} %refs_6_.3) | copy-start | bytes 12582916

commit v5 on v4

--- a/solution.py
+++ b/solution.py
@@ -20,6 +20,7 @@
 LINE = 128
 GROUP = 256
 LIMIT = 50 * 2**20
+COLUMNS_LIMIT = 50 * 2**20
 EARLY_LIMIT = 44 * 2**20
 HEIGHT_LIMIT = 36 * 2**20
 STEP = 512
@@ -36,39 +37,32 @@
     return jnp.dot(perm, x, preferred_element_type=F32).astype(BF)
 
 
-def to_columns_kernel(x_ref, o_ref, held_ref, out_ref, sems, out_sems):
+def to_columns_kernel(x_ref, o_ref, held_ref, sems):
     copies = [
         pltpu.make_async_copy(x_ref.at[:, pl.ds(2 * t, 2)], held_ref.at[t], sems.at[t])
         for t in range(4)
     ]
     for copy in copies:
         copy.start()
-    outs = []
     for t, copy in enumerate(copies):
         copy.wait()
         y = reorder(
             lambda o: (o % 4) * 64 + ((o // 4) % 2) * 32 + o // 8, held_ref[t].reshape(GROUP, D)
         )
-        out_ref[t] = y.reshape(32, 8, D)
-        outs.append(pltpu.make_async_copy(out_ref.at[t], o_ref.at[:, t], out_sems.at[t]))
-        outs[-1].start()
-    for copy in outs:
-        copy.wait()
+        o_ref[:, t] = y.reshape(32, 8, D)
 
 
 def to_columns(video):
     return pl.pallas_call(
         to_columns_kernel,
         in_specs=[pl.BlockSpec(memory_space=pltpu.HBM)],
-        out_specs=pl.BlockSpec(memory_space=pltpu.HBM),
+        out_specs=pl.BlockSpec(memory_space=pltpu.VMEM),
         out_shape=jax.ShapeDtypeStruct((32, 4, 8, D), BF),
         scratch_shapes=[
             pltpu.VMEM((4, 4, 2, 32, D), BF),
-            pltpu.VMEM((4, 32, 8, D), BF),
-            pltpu.SemaphoreType.DMA((4,)),
             pltpu.SemaphoreType.DMA((4,)),
         ],
-        compiler_params=pltpu.CompilerParams(vmem_limit_bytes=60 * 2**20),
+        compiler_params=pltpu.CompilerParams(vmem_limit_bytes=COLUMNS_LIMIT),
         name="to_columns",
     )(video)
 
@@ -308,7 +302,7 @@
     )[0]
 
 
-UNROLL = 4
+UNROLL = 8
 
 
 def on_device(video, w_triple, w_out):
@@ -321,6 +315,7 @@
     second = 64 + (s // 2) * 32 + (m % 4) * 8 + (s % 2) * 4 + r
     perm1 = permutation((m // 4) * LINE + jnp.where(chunk == 0, first, second), o)
 
+    video, perm0, perm1 = lax.optimization_barrier((video, perm0, perm1))
     lines = lax.all_to_all(to_columns(video), "mem", split_axis=0, concat_axis=0, tiled=True)
     pieces = []
     for k in range(2):

time: 128 us -> 124 us (0.969)
  blocking collectives: 36.9 us -> 73.9 us
  waiting for transfers between devices: 32.9 us -> 4.05 us
  starting transfers between devices: 17.1 us -> 6.42 us
  Pallas kernels: 40.2 us -> 38.9 us
    all_to_all x0 -> x1, blocking collectives: none -> 39.9 us  [on_device(): lax.all_to_all(to_columns(video), 'mem', split_axis=0, concat_axis=0, til...]
    all_to_all x1 -> x0, waiting for transfers between devices: 29.1 us -> none  [on_device(): lax.all_to_all(to_columns(video), 'mem', split_axis=0, concat_axis=0, til...]
    all_to_all x1 -> x0, starting transfers between devices: 11.4 us -> none  [on_device(): lax.all_to_all(to_columns(video), 'mem', split_axis=0, concat_axis=0, til...]
    all_to_all x1, blocking collectives: 36.9 us -> 34 us  [on_device(): lax.all_to_all(done.reshape(128, 8, D), ('mem', 'grp'), split_axis=0, con...]
  transfers between devices with their start and end apart: 7 -> 6, of which waited for: 3 -> 2; matrix products, arithmetic and copies ran while one was open for 0% -> 0% of each run, Pallas kernels for 13% -> 14%
where the time goes in v5:
time: 124 us
  blocking collectives  73.9 us (60%)
  Pallas kernels  38.9 us (31%)
  starting transfers between devices  6.42 us (5%)
  waiting for transfers between devices  4.05 us (3%)
    all_to_all x1, blocking collectives, on_device(): lax.all_to_all(to_columns(video), 'mem', split_axis=0, concat_axis=0, til...  39.9 us
    pallas_call x4, Pallas kernels, call(): pl.pallas_call(kernel, in_specs=[pl.BlockSpec(memory_space=pltpu.VMEM)] *...  35 us
    all_to_all x1, blocking collectives, on_device(): lax.all_to_all(done.reshape(128, 8, D), ('mem', 'grp'), split_axis=0, con...  34 us
    ppermute x6, starting transfers between devices, on_device(): lax.ppermute(outs[s], 'grp', [(i, i ^ s) for i in range(4)])  6.42 us
    ppermute x6, waiting for transfers between devices, on_device(): lax.ppermute(outs[s], 'grp', [(i, i ^ s) for i in range(4)])  4.05 us
  transfers between devices with their start and end apart: 6, of which 2 were waited for; matrix products, arithmetic and copies ran while one was open for 0% of the time, Pallas kernels for 14%

profile of v5, /device:TPU:1, one launch (start us, length us, event | category | flops | bytes accessed | tf_op | source)
XLA Modules:
  0.0 123.8 jit_solution(10414537613401258664)
XLA Ops:
  0.0 0.1 fusion.perm_ref
  0.1 0.1 fusion.1.refs_0_
  0.2 2.3 %to_columns.1 = bf16[32,4,8,1024]{3,2,1,0:T(8,128)(2,1)S(1)} custom-call(bf16[4,8,32,1024]{3,2,1,0:T(8,128)(2,1)} %x_ref), custom_call_target="tpu_custom_call" | custom-call | tf_op jit(solution)/shard_map/to_columns/pallas_call | solution.py:56
  2.5 39.9 %all_to_all.10.x_ref = bf16[32,4,8,1024]{3,2,1,0:T(8,128)(2,1)S(1)} all-to-all(bf16[32,4,8,1024]{3,2,1,0:T(8,128)(2,1)S(1)} %to_columns.1), channel_id=1, replica_groups=mesh['grp'=4,'mem'=32] {'mem'}, dimensions={0} | all-to-all | bytes 4194304 | tf_op jit(solution)/shard_map/all_to_all | solution.py:319
  42.5 8.6 %time_block_0.1 = (bf16[4,32,1024]{2,1,0:T(8,128)(2,1)S(1)}, bf16[4,32,1024]{2,1,0:T(8,128)(2,1)S(1)}, bf16[4,32,1024]{2,1,0:T(8,128)(2,1)S(1)}, bf16[4,32,1024]{2,1,0:T(8,128)(2,1)S(1)}) custom-call(bf16[256,256]{1,0:T(8,128)(2,1)S(1)} %fusion.perm_ref, bf16[32,4,8,1024]{3,2,1,0:T(8,128)(2,1)S(1)} %all_to_all.10.x_ref, bf16[2,1024,3072]{2,1,0:T(8,128)(2,1)} %refs_5_.1, ...), custom_call_target="tpu_custom_call" | custom-call | flops 4563402752 | bytes 8388608 | tf_op jit(solution)/shard_map/time_block_0/pallas_call | solution.py:156
  51.1 2.5 %collective-permute-start = (bf16[4,32,1024]{2,1,0:T(8,128)(2,1)S(1)}, bf16[4,32,1024]{2,1,0:T(8,128)(2,1)S(1)}, u32[]{:S(2)}, u32[]{:S(2)}) collective-permute-start(bf16[4,32,1024]{2,1,0:T(8,128)(2,1)S(1)} %get-tuple-element.25), channel_id=1, source_target_pairs={{0,32},{32,0},{64,96},{96,64},{1,33},{33,1},{65,97},{97,65},{2,34}... | collective-permute-start | bytes 786440 | tf_op jit(solution)/shard_map/ppermute | solution.py:325
  53.6 0.4 collective-permute-start.1
  54.0 1.3 %collective-permute-start.2 = (bf16[4,32,1024]{2,1,0:T(8,128)(2,1)S(1)}, bf16[4,32,1024]{2,1,0:T(8,128)(2,1)S(1)}, u32[]{:S(2)}, u32[]{:S(2)}) collective-permute-start(bf16[4,32,1024]{2,1,0:T(8,128)(2,1)S(1)} %get-tuple-element.27), channel_id=1, source_target_pairs={{0,96},{32,64},{64,32},{96,0},{1,97},{33,65},{65,33},{97,1},{2,98}... | collective-permute-start | bytes 786440 | tf_op jit(solution)/shard_map/ppermute | solution.py:325
  55.3 8.6 %time_block_1.1 = (bf16[4,32,1024]{2,1,0:T(8,128)(2,1)S(1)}, bf16[4,32,1024]{2,1,0:T(8,128)(2,1)S(1)}, bf16[4,32,1024]{2,1,0:T(8,128)(2,1)S(1)}, bf16[4,32,1024]{2,1,0:T(8,128)(2,1)S(1)}) custom-call(bf16[256,256]{1,0:T(8,128)(2,1)S(1)} %fusion.perm_ref, bf16[32,4,8,1024]{3,2,1,0:T(8,128)(2,1)S(1)} %all_to_all.10.x_ref, bf16[2,1024,3072]{2,1,0:T(8,128)(2,1)} %refs_5_.1, ...), custom_call_target="tpu_custom_call" | custom-call | flops 4563402752 | bytes 8388608 | tf_op jit(solution)/shard_map/time_block_1/pallas_call | solution.py:156
  63.9 0.2 collective-permute-start.3
  64.1 0.4 collective-permute-start.4
  64.5 0.0 collective-permute-done.refs_1_
  64.5 1.6 %collective-permute-start.5 = (bf16[4,32,1024]{2,1,0:T(8,128)(2,1)S(1)}, bf16[4,32,1024]{2,1,0:T(8,128)(2,1)S(1)}, u32[]{:S(2)}, u32[]{:S(2)}) collective-permute-start(bf16[4,32,1024]{2,1,0:T(8,128)(2,1)S(1)} %get-tuple-element.34), channel_id=1, source_target_pairs={{0,96},{32,64},{64,32},{96,0},{1,97},{33,65},{65,33},{97,1},{2,98}... | collective-permute-start | bytes 786440 | tf_op jit(solution)/shard_map/ppermute | solution.py:325
  66.1 0.0 collective-permute-done.1.refs_2_
  66.1 1.6 %collective-permute-done.2.refs_3_ = bf16[4,32,1024]{2,1,0:T(8,128)(2,1)S(1)} collective-permute-done((bf16[4,32,1024]{2,1,0:T(8,128)(2,1)S(1)}, bf16[4,32,1024]{2,1,0:T(8,128)(2,1)S(1)}, u32[]{:S(2)}, u32[]{:S(2)}) %collective-permute-start.2) | collective-permute-done | bytes 262176 | tf_op jit(solution)/shard_map/ppermute | solution.py:325
  67.7 0.0 collective-permute-done.3.refs_5_
  67.7 0.0 copy-start
  67.7 8.3 %early.1 = (bf16[768,3072]{1,0:T(8,128)(2,1)S(1)}, bf16[768,1024]{1,0:T(8,128)(2,1)S(1)}) custom-call(bf16[4,32,1024]{2,1,0:T(8,128)(2,1)S(1)} %get-tuple-element.24.refs_0_, bf16[4,32,1024]{2,1,0:T(8,128)(2,1)S(1)} %collective-permute-done.refs_1_, bf16[4,32,1024]{2,1,0:T(8,128)(2,1)S(1)} %collective-permute-done.1.refs_2_, ...), custom_call_target="tpu_custom_call" | custom-call | flops 4831838208 | bytes 6291456 | tf_op jit(solution)/shard_map/early/pallas_call | solution.py:156
  76.0 0.0 collective-permute-done.4.refs_3_
  76.0 2.5 %collective-permute-done.5.refs_4_ = bf16[4,32,1024]{2,1,0:T(8,128)(2,1)S(1)} collective-permute-done((bf16[4,32,1024]{2,1,0:T(8,128)(2,1)S(1)}, bf16[4,32,1024]{2,1,0:T(8,128)(2,1)S(1)}, u32[]{:S(2)}, u32[]{:S(2)}) %collective-permute-start.5) | collective-permute-done | bytes 262176 | tf_op jit(solution)/shard_map/ppermute | solution.py:325
  78.5 0.0 copy-done
  78.5 9.5 %height_block.1 = bf16[32,32,1024]{2,1,0:T(8,128)(2,1)S(1)} custom-call(bf16[256,256]{1,0:T(8,128)(2,1)S(1)} %fusion.1.refs_0_, bf16[768,3072]{1,0:T(8,128)(2,1)S(1)} %get-tuple-element.31.refs_1_, bf16[768,1024]{1,0:T(8,128)(2,1)S(1)} %get-tuple-element.32.refs_2_, bf16[4,32,1024]{2,1,0:T(8,128)(2,1)S(1)} %collective-permute-done.4.refs_3_, ...), custom_call_target="tpu_custom_call" | custom-call | flops 6979321856 | bytes 6291456 | tf_op jit(solution)/shard_map/height_block/pallas_call | solution.py:156
  88.0 34.0 %all_to_all.11 = bf16[128,8,1024]{2,1,0:T(8,128)(2,1)S(1)} all-to-all(bf16[128,8,1024]{2,1,0:T(8,128)(2,1)S(1)} %bitcast.3), channel_id=1, replica_groups=mesh['grp'=4,'mem'=32] {'mem','grp'}, dimensions={0} | all-to-all | bytes 4194304 | tf_op jit(solution)/shard_map/all_to_all | solution.py:331
  121.9 1.6 %to_tokens.1 = bf16[4,8,32,1024]{3,2,1,0:T(8,128)(2,1)} custom-call(bf16[32,4,8,1024]{3,2,1,0:T(8,128)(2,1)S(1)} %bitcast.2), custom_call_target="tpu_custom_call" | custom-call | tf_op jit(solution)/shard_map/to_tokens/pallas_call | solution.py:82
  (1 shorter events, 0.0 us)
Async XLA Ops:
  51.1 13.4 %collective-permute-start = (bf16[4,32,1024]{2,1,0:T(8,128)(2,1)S(1)}, bf16[4,32,1024]{2,1,0:T(8,128)(2,1)S(1)}, u32[]{:S(2)}, u32[]{:S(2)}) collective-permute-start(bf16[4,32,1024]{2,1,0:T(8,128)(2,1)S(1)} %get-tuple-element.25), channel_id=1, source_target_pairs={{0,32},{32,0},{64,96},{96,64},{1,33},{33,1},{65,97},{97,65},{2,34}... | collective-permute-start | bytes 786440 | tf_op jit(solution)/shard_map/ppermute | solution.py:325
  53.6 12.6 %collective-permute-start.1 = (bf16[4,32,1024]{2,1,0:T(8,128)(2,1)S(1)}, bf16[4,32,1024]{2,1,0:T(8,128)(2,1)S(1)}, u32[]{:S(2)}, u32[]{:S(2)}) collective-permute-start(bf16[4,32,1024]{2,1,0:T(8,128)(2,1)S(1)} %get-tuple-element.26), channel_id=1, source_target_pairs={{0,64},{32,96},{64,0},{96,32},{1,65},{33,97},{65,1},{97,33},{2,66}... | collective-permute-start | bytes 786440 | tf_op jit(solution)/shard_map/ppermute | solution.py:325
  54.0 13.7 %collective-permute-start.2 = (bf16[4,32,1024]{2,1,0:T(8,128)(2,1)S(1)}, bf16[4,32,1024]{2,1,0:T(8,128)(2,1)S(1)}, u32[]{:S(2)}, u32[]{:S(2)}) collective-permute-start(bf16[4,32,1024]{2,1,0:T(8,128)(2,1)S(1)} %get-tuple-element.27), channel_id=1, source_target_pairs={{0,96},{32,64},{64,32},{96,0},{1,97},{33,65},{65,33},{97,1},{2,98}... | collective-permute-start | bytes 786440 | tf_op jit(solution)/shard_map/ppermute | solution.py:325
  63.9 3.8 %collective-permute-start.3 = (bf16[4,32,1024]{2,1,0:T(8,128)(2,1)S(1)}, bf16[4,32,1024]{2,1,0:T(8,128)(2,1)S(1)}, u32[]{:S(2)}, u32[]{:S(2)}) collective-permute-start(bf16[4,32,1024]{2,1,0:T(8,128)(2,1)S(1)} %get-tuple-element.30), channel_id=1, source_target_pairs={{0,32},{32,0},{64,96},{96,64},{1,33},{33,1},{65,97},{97,65},{2,34}... | collective-permute-start | bytes 786440 | tf_op jit(solution)/shard_map/ppermute | solution.py:325
  64.1 11.8 %collective-permute-start.4 = (bf16[4,32,1024]{2,1,0:T(8,128)(2,1)S(1)}, bf16[4,32,1024]{2,1,0:T(8,128)(2,1)S(1)}, u32[]{:S(2)}, u32[]{:S(2)}) collective-permute-start(bf16[4,32,1024]{2,1,0:T(8,128)(2,1)S(1)} %get-tuple-element.33), channel_id=1, source_target_pairs={{0,64},{32,96},{64,0},{96,32},{1,65},{33,97},{65,1},{97,33},{2,66}... | collective-permute-start | bytes 786440 | tf_op jit(solution)/shard_map/ppermute | solution.py:325
  64.5 13.9 %collective-permute-start.5 = (bf16[4,32,1024]{2,1,0:T(8,128)(2,1)S(1)}, bf16[4,32,1024]{2,1,0:T(8,128)(2,1)S(1)}, u32[]{:S(2)}, u32[]{:S(2)}) collective-permute-start(bf16[4,32,1024]{2,1,0:T(8,128)(2,1)S(1)} %get-tuple-element.34), channel_id=1, source_target_pairs={{0,96},{32,64},{64,32},{96,0},{1,97},{33,65},{65,33},{97,1},{2,98}... | collective-permute-start | bytes 786440 | tf_op jit(solution)/shard_map/ppermute | solution.py:325
  67.7 10.8 %copy-start = (bf16[2,1024,1024]{2,1,0:T(8,128)(2,1)S(1)}, bf16[2,1024,1024]{2,1,0:T(8,128)(2,1)}, u32[]{:S(2)}) copy-start(bf16[2,1024,1024]{2,1,0:T(8,128)(2,1)} %refs_6_.3) | copy-start | bytes 12582916
